TPU v7x, 32 devices: a whole 2x2x4 slice. The times are simulated.
32 devices in a mesh: dp: 8 (over y, x, core), seq: 4 (over z).
Axes of the slice: x: 2, y: 2, z: 4, core: 2. Of those that a mesh axis runs over, the one named last changes fastest.
Arguments:
- patches: bfloat16 [96, 576, 384], P('dp', 'seq'), may hold values from -6 to 6
- first_gain: bfloat16 [384], replicated, may hold values from 0.5 to 1.5
- first_shift: bfloat16 [384], replicated, may hold values from -1.25 to 1.25
- qkv_weight: bfloat16 [384, 1152], replicated, may hold values from -0.3125 to 0.3125
- query_value_bias: bfloat16 [768], replicated, may hold values from -1.75 to 1.75
- out_weight: bfloat16 [384, 384], replicated, may hold values from -2.5 to 2.5
- out_bias: bfloat16 [384], replicated, may hold values from -1.25 to 1.25
- second_gain: bfloat16 [384], replicated, may hold values from 0.5 to 1.5
- second_shift: bfloat16 [384], replicated, may hold values from -1.25 to 1.25
- up_weight: bfloat16 [384, 1536], replicated, may hold values from -0.3125 to 0.3125
- up_bias: bfloat16 [1536], replicated, may hold values from -1.75 to 1.75
- down_weight: bfloat16 [1536, 384], replicated, may hold values from -0.15625 to 0.15625
- down_bias: bfloat16 [384], replicated, may hold values from -1.25 to 1.25
- map_weight: bfloat16 [384, 8], replicated, may hold values from -0.3125 to 0.3125
- map_bias: bfloat16 [8], replicated, may hold values from -3 to 3
- keep_mask: int32 [96, 576], P('dp', 'seq'), may hold values from 0 to 1, as said below
- image_valid: int32 [96], P('dp'), may hold values from 0 to 1, as said below
- token_cotangent: bfloat16 [96, 8, 384], P('dp'), may hold values from -448 to 448
Outputs:
- learned: float32 [96, 8, 384], P('dp')
- penalty: float32 [], replicated
- grad_patches: float32 [96, 576, 384], P('dp', 'seq')
- grad_first_gain: float32 [384], replicated
- grad_first_shift: float32 [384], replicated
- grad_qkv_weight: float32 [384, 1152], replicated
- grad_query_value_bias: float32 [768], replicated
- grad_out_weight: float32 [384, 384], replicated
- grad_out_bias: float32 [384], replicated
- grad_second_gain: float32 [384], replicated
- grad_second_shift: float32 [384], replicated
- grad_up_weight: float32 [384, 1536], replicated
- grad_up_bias: float32 [1536], replicated
- grad_down_weight: float32 [1536, 384], replicated
- grad_down_bias: float32 [384], replicated
- grad_map_weight: float32 [384, 8], replicated
- grad_map_bias: float32 [8], replicated
Inputs may be any that keep to these rules, and one draw needn't show every extreme that they name: `keep_mask`: patch 0 of every image is kept. `image_valid`: the last image is valid.
All inputs are finite; a program needn't handle non-finite values.
Results may differ from a plain program's by a relative error of at most 0.0049.
Values may be sent and summed in bfloat16 or wider, within the bound.
No kernel may reach another device: no remote copies, remote signals or barrier semaphores. Data moves between devices by JAX's collectives and lax.ppermute only.
A program may use at most 256 MiB of HBM per device.

v0:
```python
import functools
import math

import jax
import jax.numpy as jnp
from jax import lax
from jax.sharding import PartitionSpec as P

HEADS = 6
HD = 64


PRECISE = lax.Precision.HIGHEST
EPSILON = 1e-06
MASKED_SCORE = -1e30


def layer_norm(values, scale_vec, shift_vec):
    average = jnp.mean(values, axis=-1, keepdims=True)
    centred = values - average
    variance = jnp.mean(centred * centred, axis=-1, keepdims=True)
    return centred * lax.rsqrt(variance + EPSILON) * scale_vec + shift_vec


def exact_gelu(values):
    return jax.nn.gelu(values, approximate=False)


def by_blocks(function, image_count, row_count, tensors):
    block_images = math.gcd(image_count, max(1, -(-512 // row_count)))
    blocked = tuple(
        (
            tensor.reshape((image_count // block_images, block_images) + tensor.shape[1:])
            for tensor in tensors
        )
    )
    results = lax.map(lambda pieces: function(*pieces), blocked)
    return tuple((result.reshape((image_count,) + result.shape[2:]) for result in results))


def attend_block(queries, keys_low, values, keep_rows):
    scale_factor = queries.shape[-1] ** (-0.5)
    scores = (
        jnp.einsum("gqhe,gkhe->ghqk", queries, keys_low, preferred_element_type=jnp.float32)
        * scale_factor
    )
    scores = jnp.where(keep_rows[:, None, None, :], scores, MASKED_SCORE)
    row_max = jnp.max(scores, axis=-1, keepdims=True)
    exponent = jnp.exp(scores - row_max)
    row_total = jnp.sum(exponent, axis=-1, keepdims=True)
    probabilities = (exponent / row_total).astype(jnp.bfloat16)
    attended = jnp.einsum(
        "ghqk,gkhe->gqhe", probabilities, values, preferred_element_type=jnp.float32
    )
    return (attended, (row_max + jnp.log(row_total))[..., 0])


def attend_grad(queries, keys_low, values, keep_rows, log_total, grad_att):
    scale_factor = queries.shape[-1] ** (-0.5)
    scores = (
        jnp.einsum("gqhe,gkhe->ghqk", queries, keys_low, preferred_element_type=jnp.float32)
        * scale_factor
    )
    scores = jnp.where(keep_rows[:, None, None, :], scores, MASKED_SCORE)
    probabilities = jnp.exp(scores - log_total[..., None])
    grad_probs = jnp.einsum("gqhe,gkhe->ghqk", grad_att, values, preferred_element_type=jnp.float32)
    row_delta = jnp.sum(probabilities * grad_probs, axis=-1, keepdims=True)
    grad_scores = (probabilities * (grad_probs - row_delta) * scale_factor).astype(jnp.bfloat16)
    grad_query = jnp.einsum(
        "ghqk,gkhe->gqhe", grad_scores, keys_low, preferred_element_type=jnp.float32
    )
    grad_key = jnp.einsum(
        "ghqk,gqhe->gkhe", grad_scores, queries, preferred_element_type=jnp.float32
    )
    grad_value = jnp.einsum(
        "ghqk,gqhe->gkhe",
        probabilities.astype(jnp.bfloat16),
        grad_att,
        preferred_element_type=jnp.float32,
    )
    return (grad_query, grad_key, grad_value)


def learner_terms(output, map_matrix, map_offset, kept_float):
    logits = jnp.einsum("gpd,ds->gps", output, map_matrix, precision=PRECISE) + map_offset
    token_maps = jax.nn.sigmoid(logits)
    weighted = token_maps * kept_float[..., None]
    token_sums = jnp.einsum("gps,gpd->gsd", weighted, output, precision=PRECISE)
    map_total = jnp.sum(token_maps, axis=-1)
    intersection = jnp.sum(
        kept_float * (map_total * map_total - jnp.sum(token_maps * token_maps, axis=-1)), axis=1
    )
    return (token_sums, intersection)


def per_device(
    patches,
    first_gain,
    first_shift,
    qkv_weight,
    query_value_bias,
    out_weight,
    out_bias,
    second_gain,
    second_shift,
    up_weight,
    up_bias,
    down_weight,
    down_bias,
    map_weight,
    map_bias,
    keep_mask,
    image_valid,
    token_cotangent,
):
    images, part_rows, features = patches.shape
    seq_parts = lax.axis_size("seq")
    image_patches = float(part_rows * seq_parts)
    keep_low = keep_mask.astype(jnp.bfloat16)
    cot_all = token_cotangent.astype(jnp.float32)
    valid_all = image_valid.astype(jnp.float32)
    rows_in, keep_in, cot_in, valid_in = (patches, keep_low, cot_all, valid_all)
    length = rows_in.shape[1]
    inputs = rows_in.astype(jnp.float32)
    normed, first_back = jax.vjp(
        layer_norm, inputs, first_gain.astype(jnp.float32), first_shift.astype(jnp.float32)
    )
    normed_low = normed.astype(jnp.bfloat16)
    mixed_rows = jnp.einsum(
        "gpd,de->gpe", normed_low, qkv_weight, preferred_element_type=jnp.float32
    )
    bias_float = query_value_bias.astype(jnp.float32)
    queries = (mixed_rows[..., :features] + bias_float[:features]).astype(jnp.bfloat16)
    keys_low = mixed_rows[..., features : 2 * features].astype(jnp.bfloat16)
    values = (mixed_rows[..., 2 * features :] + bias_float[features:]).astype(jnp.bfloat16)
    all_keys, all_values, all_keep = (
        lax.all_gather(keys_low, "seq", axis=1, tiled=True),
        lax.all_gather(values, "seq", axis=1, tiled=True),
        lax.all_gather(keep_in, "seq", axis=1, tiled=True),
    )
    full_rows = all_keys.shape[1]
    query_heads = queries.reshape(images, length, HEADS, HD)
    key_heads = all_keys.reshape(images, full_rows, HEADS, HD)
    value_heads = all_values.reshape(images, full_rows, HEADS, HD)
    keep_bool = all_keep > 0.5
    attended, log_total = by_blocks(
        attend_block, images, length, (query_heads, key_heads, value_heads, keep_bool)
    )
    att_low = attended.reshape(images, length, features).astype(jnp.bfloat16)
    middle = (
        inputs
        + jnp.einsum("gpe,ed->gpd", att_low, out_weight, preferred_element_type=jnp.float32)
        + out_bias.astype(jnp.float32)
    )
    second_normed, second_back = jax.vjp(
        layer_norm, middle, second_gain.astype(jnp.float32), second_shift.astype(jnp.float32)
    )
    second_low = second_normed.astype(jnp.bfloat16)
    hidden_pre = jnp.einsum(
        "gpd,df->gpf", second_low, up_weight, preferred_element_type=jnp.float32
    ) + up_bias.astype(jnp.float32)
    activated, gelu_back = jax.vjp(exact_gelu, hidden_pre)
    hidden_low = activated.astype(jnp.bfloat16)
    output = (
        middle
        + jnp.einsum("gpf,fd->gpd", hidden_low, down_weight, preferred_element_type=jnp.float32)
        + down_bias.astype(jnp.float32)
    )
    kept_float = keep_in.astype(jnp.float32)
    (token_sums, intersection), learner_back = jax.vjp(
        functools.partial(learner_terms, kept_float=kept_float),
        output,
        map_weight.astype(jnp.float32),
        map_bias.astype(jnp.float32),
    )
    counts = jnp.sum(kept_float, axis=1)
    token_sums, intersection, counts = lax.psum((token_sums, intersection, counts), "seq")
    learned = token_sums / counts[:, None, None]
    penalty_share = jnp.sum(valid_in * intersection) / image_patches
    valid_count = jnp.sum(valid_in)
    penalty_share, valid_count = lax.psum((penalty_share, valid_count), "dp")
    penalty = penalty_share / valid_count
    grad_sums = cot_in / counts[:, None, None]
    grad_intersection = valid_in / valid_count
    grad_output, grad_map_weight, grad_map_bias = learner_back((grad_sums, grad_intersection))
    grad_down_bias = jnp.sum(grad_output, axis=(0, 1))
    grad_out_low = grad_output.astype(jnp.bfloat16)
    grad_down_weight = jnp.einsum(
        "gpf,gpd->fd", hidden_low, grad_out_low, preferred_element_type=jnp.float32
    )
    grad_hidden = jnp.einsum(
        "gpd,fd->gpf", grad_out_low, down_weight, preferred_element_type=jnp.float32
    ).astype(jnp.bfloat16)
    (grad_pre,) = gelu_back(grad_hidden.astype(jnp.float32))
    grad_up_bias = jnp.sum(grad_pre, axis=(0, 1))
    grad_pre_low = grad_pre.astype(jnp.bfloat16)
    grad_up_weight = jnp.einsum(
        "gpd,gpf->df", second_low, grad_pre_low, preferred_element_type=jnp.float32
    )
    grad_second = jnp.einsum(
        "gpf,df->gpd", grad_pre_low, up_weight, preferred_element_type=jnp.float32
    )
    grad_middle_norm, grad_second_gain, grad_second_shift = second_back(grad_second)
    grad_middle = grad_output + grad_middle_norm
    grad_out_bias = jnp.sum(grad_middle, axis=(0, 1))
    grad_middle_low = grad_middle.astype(jnp.bfloat16)
    grad_out_weight = jnp.einsum(
        "gpe,gpd->ed", att_low, grad_middle_low, preferred_element_type=jnp.float32
    )
    grad_att = jnp.einsum(
        "gpd,ed->gpe", grad_middle_low, out_weight, preferred_element_type=jnp.float32
    ).astype(jnp.bfloat16)
    grad_att_heads = grad_att.reshape(images, length, HEADS, HD)
    grad_query, grad_key_all, grad_value_all = by_blocks(
        attend_grad,
        images,
        length,
        (query_heads, key_heads, value_heads, keep_bool, log_total, grad_att_heads),
    )
    grad_key_all = grad_key_all.reshape(images, full_rows, features)
    grad_value_all = grad_value_all.reshape(images, full_rows, features)
    grad_key, grad_value = (
        lax.psum_scatter(grad_key_all, "seq", scatter_dimension=1, tiled=True),
        lax.psum_scatter(grad_value_all, "seq", scatter_dimension=1, tiled=True),
    )
    grad_query = grad_query.reshape(images, length, features)
    grad_query_value_bias = jnp.concatenate(
        [jnp.sum(grad_query, axis=(0, 1)), jnp.sum(grad_value, axis=(0, 1))]
    )
    grad_mixed = jnp.concatenate([grad_query, grad_key, grad_value], axis=-1).astype(jnp.bfloat16)
    grad_qkv_weight = jnp.einsum(
        "gpd,gpe->de", normed_low, grad_mixed, preferred_element_type=jnp.float32
    )
    grad_first = jnp.einsum(
        "gpe,de->gpd", grad_mixed, qkv_weight, preferred_element_type=jnp.float32
    )
    grad_input_norm, grad_first_gain, grad_first_shift = first_back(grad_first)
    grad_inputs = grad_middle + grad_input_norm
    summed = lax.psum(
        (
            grad_first_gain,
            grad_first_shift,
            grad_qkv_weight,
            grad_query_value_bias,
            grad_out_weight,
            grad_out_bias,
            grad_second_gain,
            grad_second_shift,
            grad_up_weight,
            grad_up_bias,
            grad_down_weight,
            grad_down_bias,
            grad_map_weight,
            grad_map_bias,
        ),
        ("dp", "seq"),
    )
    return (learned, penalty, grad_inputs) + tuple(summed)


def solution(mesh):
    placed = (
        P("dp", "seq", None),
        P(),
        P(),
        P(),
        P(),
        P(),
        P(),
        P(),
        P(),
        P(),
        P(),
        P(),
        P(),
        P(),
        P(),
        P("dp", "seq"),
        P("dp"),
        P("dp", None, None),
    )
    return jax.shard_map(
        per_device,
        mesh=mesh,
        in_specs=placed,
        out_specs=(
            P("dp", None, None),
            P(),
            P("dp", "seq", None),
            P(),
            P(),
            P(),
            P(),
            P(),
            P(),
            P(),
            P(),
            P(),
            P(),
            P(),
            P(),
            P(),
            P(),
        ),
        check_vma=False,
    )
```

profile of v0, /device:TPU:0, one launch (start us, length us, event | category | flops | bytes accessed | tf_op | source)
XLA Modules:
  0.0 1241.5 jit_solution(11779511866614657590)
XLA Ops:
  13.3 4.1 fusion.135
  17.4 3.1 copy-done.5
  21.9 4.5 fusion.116
  30.0 17.2 %all-gather = bf16[4,144,12]{1,2,0:T(8,128)(2,1)S(1)} all-gather(bf16[1,144,12]{1,2,0:T(8,128)(2,1)S(1)} %bitcast.195), channel_id=1, replica_groups=mesh['dp'=8,'seq'=4] {'seq'}, dimensions={0}, use_global_device_ids=true | all-gather | bytes 17280 | tf_op jit(solution)/shard_map/all_gather | solution.py:139
  47.9 2.6 copy.69
  52.2 71.8 %all-gather.6.cloned.1.call-done = bf16[12,576,384]{2,1,0:T(8,128)(2,1)} async-done(((bf16[12,144,384]{2,1,0:T(8,128)(2,1)}), bf16[12,576,384]{2,1,0:T(8,128)(2,1)}) %all-gather.6.cloned.1.call-update) | async-done | bytes 5308432 | tf_op jit(solution)/shard_map/all_gather | solution.py:137
  124.1 8.7 copy.70
  132.8 90.9 %all-gather.4.cloned.1.call-done = bf16[12,576,384]{2,1,0:T(8,128)(2,1)} async-done(((bf16[12,144,384]{2,1,0:T(8,128)(2,1)}), bf16[12,576,384]{2,1,0:T(8,128)(2,1)}) %all-gather.4.cloned.1.call-update) | async-done | bytes 5308432 | tf_op jit(solution)/shard_map/all_gather | solution.py:138
  223.7 8.7 copy.67
  232.4 35.8 %while.28 = (s32[]{:T(128)}, bf16[3,4,144,6,64]{2,4,3,1,0:T(8,128)(2,1)}, f32[3,4,6,144]{3,2,1,0:T(8,128)}, bf16[3,4,576,6,64]{2,4,3,1,0:T(8,128)(2,1)}, pred[3,...) while((s32[]{:T(128)}, ...), condition=%wide.region_5.6_spmd.clone, body=%wide.region_2.5_spmd.sunk.clone | while | flops 533492352 | bytes 41862548 | solution.py:37
  233.1 3.3 fusion.215
  236.4 2.5 fusion.216
  238.9 3.9 bitcast_dynamic-update-slice_fusion.15
  244.9 3.3 fusion.215
  248.2 2.5 fusion.216
  250.7 3.9 bitcast_dynamic-update-slice_fusion.15
  256.7 3.3 fusion.215
  260.0 2.5 fusion.216
  262.4 3.9 bitcast_dynamic-update-slice_fusion.15
  268.3 3.7 fusion.169
  273.5 5.7 fusion.103
  279.3 25.5 %multiply_convert_fusion.1 = (bf16[12,144,1536]{2,1,0:T(8,128)(2,1)S(1)}, f32[12,144,1536]{2,1,0:T(8,128)}) fusion(f32[12,144,1536]{2,1,0:T(8,128)S(1)} %get-tuple-element.220, f32[1536]{0:T(1024)S(1)} %copy-done.45, u16[144,1536]{1,0:T(8,128)(2,1)S(1)} %get-tuple-element.132, u16[144,1536]{1,0:T(8,128)(2,1)S(1)} %get-tuple-element.131), kind=kLoop, calls=%fused_computation.90 | loop fusion | flops 188448768 | bytes 27432960 | tf_op jit(solution)/shard_map/convert_element_type | solution.py:163
  304.8 3.0 add_add_fusion.4
  312.9 9.4 all-reduce.3
  324.2 12.9 %all-reduce.2 = (f32[]{:T(128)}, f32[]{:T(128)}) all-reduce(f32[]{:T(128)S(6)} %div.80, f32[]{:T(128)} %get-tuple-element.145), channel_id=1, replica_groups=mesh['dp'=8,'seq'=4] {'dp'}, use_global_device_ids=true, to_apply=%region_16.17 | all-reduce | flops 2 | bytes 16 | tf_op jit(solution)/shard_map/psum | solution.py:181
  339.4 3.3 fusion.146
  342.7 4.6 fusion.171
  348.8 11.9 fusion.170
  360.8 4.1 fusion.160
  372.4 3.8 copy.72
  376.2 261.6 %while.29 = (s32[]{:T(128)}, f32[3,4,144,6,64]{2,4,3,1,0:T(8,128)}, f32[3,4,576,6,64]{2,4,3,1,0:T(8,128)}, f32[3,4,576,6,64]{2,4,3,1,0:T(8,128)}, bf16[3,4,576,6...) while((s32[]{:T(128)}, f32[3,4,144,6,64]{2,4,3,1,0:T(8,128)}, ...), condition=%wide.region_23.24_spmd.clone, body=%wide.region_21.23_spmd.sunk.clone | while | flops 1325784960 | bytes 114227576 | solution.py:37
  377.8 6.4 fusion.228
  384.1 6.5 fusion.227
  390.6 32.4 %bitcast_dynamic-update-slice_fusion.17 = f32[3,4,144,6,64]{2,4,3,1,0:T(8,128)} fusion(f32[3,4,144,6,64]{2,4,3,1,0:T(8,128)} %get-tuple-element.410, s32[]{:T(128)S(6)} %copy.99, f32[4,6,144,576]{3,2,1,0:T(8,128)} %fusion.227, f32[4,6,144,576]{3,2,1,0:T(8,128)} %fusion.228, f32[4,6,144]{2,1,0:T(8,128)S(1)} %dynamic-slice_bitcast_fusion.10, ...), kind=kOutput, calls=%fused_computation.51.clone.1.clone | convolution fusion | flops 276705216 | bytes 39000064 | tf_op jit(solution)/shard_map/while/body/eval_jaxpr/ghqk,gkhe->gqhe/dot_general | solution.py:69
  423.1 32.4 %bitcast_dynamic-update-slice_fusion.18 = f32[3,4,576,6,64]{2,4,3,1,0:T(8,128)} fusion(f32[3,4,576,6,64]{2,4,3,1,0:T(8,128)} %get-tuple-element.411, s32[]{:T(128)S(6)} %copy.99, f32[4,6,144,576]{3,2,1,0:T(8,128)} %fusion.227, f32[4,6,144,576]{3,2,1,0:T(8,128)} %fusion.228, f32[4,6,144]{2,1,0:T(8,128)S(1)} %dynamic-slice_bitcast_fusion.10, ...), kind=kOutput, calls=%fused_computation.42.clone.1.clone | convolution fusion | flops 276705216 | bytes 40179712 | tf_op jit(solution)/shard_map/while/body/eval_jaxpr/ghqk,gqhe->gkhe/dot_general | solution.py:72
  455.5 7.9 bitcast_dynamic-update-slice_fusion.19
  464.8 6.4 fusion.228
  471.2 6.5 fusion.227
  477.7 32.5 %bitcast_dynamic-update-slice_fusion.17 = f32[3,4,144,6,64]{2,4,3,1,0:T(8,128)} fusion(f32[3,4,144,6,64]{2,4,3,1,0:T(8,128)} %get-tuple-element.410, s32[]{:T(128)S(6)} %copy.99, f32[4,6,144,576]{3,2,1,0:T(8,128)} %fusion.227, f32[4,6,144,576]{3,2,1,0:T(8,128)} %fusion.228, f32[4,6,144]{2,1,0:T(8,128)S(1)} %dynamic-slice_bitcast_fusion.10, ...), kind=kOutput, calls=%fused_computation.51.clone.1.clone | convolution fusion | flops 276705216 | bytes 39000064 | tf_op jit(solution)/shard_map/while/body/eval_jaxpr/ghqk,gkhe->gqhe/dot_general | solution.py:69
  510.2 32.4 %bitcast_dynamic-update-slice_fusion.18 = f32[3,4,576,6,64]{2,4,3,1,0:T(8,128)} fusion(f32[3,4,576,6,64]{2,4,3,1,0:T(8,128)} %get-tuple-element.411, s32[]{:T(128)S(6)} %copy.99, f32[4,6,144,576]{3,2,1,0:T(8,128)} %fusion.227, f32[4,6,144,576]{3,2,1,0:T(8,128)} %fusion.228, f32[4,6,144]{2,1,0:T(8,128)S(1)} %dynamic-slice_bitcast_fusion.10, ...), kind=kOutput, calls=%fused_computation.42.clone.1.clone | convolution fusion | flops 276705216 | bytes 40179712 | tf_op jit(solution)/shard_map/while/body/eval_jaxpr/ghqk,gqhe->gkhe/dot_general | solution.py:72
  542.6 7.9 bitcast_dynamic-update-slice_fusion.19
  551.9 6.4 fusion.228
  558.2 6.5 fusion.227
  564.7 32.3 %bitcast_dynamic-update-slice_fusion.17 = f32[3,4,144,6,64]{2,4,3,1,0:T(8,128)} fusion(f32[3,4,144,6,64]{2,4,3,1,0:T(8,128)} %get-tuple-element.410, s32[]{:T(128)S(6)} %copy.99, f32[4,6,144,576]{3,2,1,0:T(8,128)} %fusion.227, f32[4,6,144,576]{3,2,1,0:T(8,128)} %fusion.228, f32[4,6,144]{2,1,0:T(8,128)S(1)} %dynamic-slice_bitcast_fusion.10, ...), kind=kOutput, calls=%fused_computation.51.clone.1.clone | convolution fusion | flops 276705216 | bytes 39000064 | tf_op jit(solution)/shard_map/while/body/eval_jaxpr/ghqk,gkhe->gqhe/dot_general | solution.py:69
  597.0 32.5 %bitcast_dynamic-update-slice_fusion.18 = f32[3,4,576,6,64]{2,4,3,1,0:T(8,128)} fusion(f32[3,4,576,6,64]{2,4,3,1,0:T(8,128)} %get-tuple-element.411, s32[]{:T(128)S(6)} %copy.99, f32[4,6,144,576]{3,2,1,0:T(8,128)} %fusion.227, f32[4,6,144,576]{3,2,1,0:T(8,128)} %fusion.228, f32[4,6,144]{2,1,0:T(8,128)S(1)} %dynamic-slice_bitcast_fusion.10, ...), kind=kOutput, calls=%fused_computation.42.clone.1.clone | convolution fusion | flops 276705216 | bytes 40179712 | tf_op jit(solution)/shard_map/while/body/eval_jaxpr/ghqk,gqhe->gkhe/dot_general | solution.py:72
  629.5 7.9 bitcast_dynamic-update-slice_fusion.19
  637.8 13.1 %copy.74 = f32[12,576,384]{2,1,0:T(8,128)} copy(f32[12,576,384]{1,2,0:T(8,128)} %bitcast.190) | data formatting | bytes 21233664 | tf_op jit(solution)/shard_map/reshape;reshape | solution.py:221
  651.0 13.3 %copy.73 = f32[12,576,384]{2,1,0:T(8,128)} copy(f32[12,576,384]{1,2,0:T(8,128)} %bitcast.191) | data formatting | bytes 21233664 | tf_op jit(solution)/shard_map/reshape;reshape | solution.py:220
  664.4 4.6 fusion.166
  671.2 4.0 fusion.148
  675.2 4.4 convolution_bitcast_fusion.3
  679.6 7.2 convolution_bitcast_fusion.1
  686.9 4.0 convolution_bitcast_fusion.2
  691.2 138.0 %reduce-scatter.5.cloned.1.call-done = f32[12,144,384]{2,1,0:T(8,128)} async-done(((f32[12,576,384]{2,1,0:T(8,128)}), f32[12,144,384]{2,1,0:T(8,128)}) %reduce-scatter.5.cloned.1.call-update) | async-done | bytes 2654224 | tf_op jit(solution)/shard_map/reduce_scatter | solution.py:224
  829.2 3.9 fusion.167
  833.2 179.6 %reduce-scatter.3.cloned.1.call-done = f32[12,144,384]{2,1,0:T(8,128)} async-done(((f32[12,576,384]{2,1,0:T(8,128)}), f32[12,144,384]{2,1,0:T(8,128)}) %reduce-scatter.3.cloned.1.call-update) | async-done | bytes 2654224 | tf_op jit(solution)/shard_map/reduce_scatter | solution.py:223
  1016.0 4.7 convolution_bitcast_fusion
  1022.2 3.2 convolution_bitcast_fusion.4
  1025.5 25.5 %all-reduce.7.cloned.1.call-done = f32[12,8,384]{2,1,0:T(8,128)} async-done(((f32[12,8,384]{2,1,0:T(8,128)}), f32[12,8,384]{2,1,0:T(8,128)}) %all-reduce.7.cloned.1.call-update) | async-done | bytes 147472 | tf_op jit(solution)/shard_map/psum | solution.py:177
  1052.6 4.5 fusion.161
  1060.4 43.6 %all-reduce = (f32[384]{0:T(512)}, f32[384]{0:T(512)}, f32[768]{0:T(1024)}, f32[384]{0:T(512)}, f32[384]{0:T(512)}, /*index=5*/f32[384]{0:T(512)}, f32[1536]{0:T...) all-reduce(f32[384]{0:T(512)S(1)} %get-tuple-element.135, ...), channel_id=1, replica_groups=mesh['dp'=8,'seq'=4] {'dp','seq'}, use_global_device_ids=true, to_apply=%region_29.30 | all-reduce | flops 7688 | bytes 61504 | tf_op jit(solution)/shard_map/psum | solution.py:239
  1104.0 4.1 add_add_fusion.2
  1108.1 117.4 %all-reduce.9.cloned.1.call-done = (f32[384,1152]{1,0:T(8,128)}, f32[384,384]{1,0:T(8,128)}, f32[384,1536]{1,0:T(8,128)}, f32[1536,384]{1,0:T(8,128)}) async-done(((f32[384,1152]{1,0:T(8,128)}, f32[384,384]{1,0:T(8,128)}, f32[384,1536]{1,0:T(8,128)}, f32[1536,384]{1,0:T(8,128)}), (f32[384,1152]{1,0:T(8,128)}, f32[384,384]{1,0:T(8,128)}, f32[384,1536]{1,0:T(8,128)}, ...) | async-done | bytes 7077904 | tf_op jit(solution)/shard_map/psum | solution.py:239
  1225.6 2.9 copy.113
  (241 shorter events, 58.4 us)
Async XLA Ops:
  7.2 266.3 %copy-start = (bf16[384,1536]{1,0:T(8,128)(2,1)S(1)}, bf16[384,1536]{1,0:T(8,128)(2,1)}, u32[]{:S(2)}) copy-start(bf16[384,1536]{1,0:T(8,128)(2,1)} %param.31) | copy-start | bytes 3538948
  7.2 116.9 %all-gather.6.cloned.1.call-start = ((), (), s32[]{:S(2)}) async-start(), calls=%async_computation.3 | async-start | bytes 6635520 | tf_op jit(solution)/shard_map/all_gather | solution.py:137
  8.0 9.3 copy-start.47
  8.7 8.7 copy-start.56
  10.5 6.9 copy-start.25
  13.3 4.1 copy-start.28
  21.7 202.0 %all-gather.4.cloned.1.call-start = ((), (), s32[]{:S(2)}) async-start(), calls=%async_computation.2 | async-start | bytes 6635520 | tf_op jit(solution)/shard_map/all_gather | solution.py:138
  21.8 4.7 copy-start.76
  21.8 5.2 copy-start.69
  21.8 5.8 copy-start.70
  21.8 6.4 copy-start.71
  21.8 6.9 copy-start.72
  21.9 7.5 copy-start.63
  21.9 8.1 copy-start.54
  26.4 802.8 %reduce-scatter.5.cloned.1.call-start = ((), (), s32[]{:S(2)}) async-start(), calls=%async_computation.6 | async-start | bytes 13271040 | tf_op jit(solution)/shard_map/reduce_scatter | solution.py:224
  30.0 17.2 %copy-start.43 = (bf16[12,144]{1,0:T(8,128)(2,1)}, bf16[12,144]{1,0:T(8,128)(2,1)S(1)}, u32[]{:S(2)}) copy-start(bf16[12,144]{1,0:T(8,128)(2,1)S(1)} %get-tuple-element.202) | copy-start | bytes 10372
  30.0 312.7 %copy-start.30 = (f32[12,144]{1,0:T(8,128)}, f32[12,144]{1,0:T(8,128)S(1)}, u32[]{:S(2)}) copy-start(f32[12,144]{1,0:T(8,128)S(1)} %get-tuple-element.201) | copy-start | bytes 20740
  268.2 5.3 copy-start.45
  268.2 5.3 copy-start.51
  268.2 5.3 copy-start.65
  272.0 32.8 %copy-start.7 = (f32[12,144,384]{2,1,0:T(8,128)}, f32[12,144,384]{2,1,0:T(8,128)S(1)}, u32[]{:S(2)}) copy-start(f32[12,144,384]{2,1,0:T(8,128)S(1)} %get-tuple-element.219) | copy-start | bytes 7962628
  272.0 7.2 copy-start.32
  273.5 5.7 copy-start.35
  279.2 25.5 %copy-start.11 = (f32[12,144,1536]{2,1,0:T(8,128)}, f32[12,144,1536]{2,1,0:T(8,128)S(1)}, u32[]{:S(2)}) copy-start(f32[12,144,1536]{2,1,0:T(8,128)S(1)} %get-tuple-element.220) | copy-start | bytes 31850500
  279.2 25.5 %copy-start.67 = (f32[384]{0:T(512)S(1)}, f32[384]{0:T(512)}, u32[]{:S(2)}) copy-start(f32[384]{0:T(512)} %convert_element_type.109) | copy-start | bytes 4612
  279.2 25.5 %copy-start.74 = (bf16[1536,384]{1,0:T(8,128)(2,1)S(1)}, bf16[1536,384]{1,0:T(8,128)(2,1)}, u32[]{:S(2)}) copy-start(bf16[1536,384]{1,0:T(8,128)(2,1)} %param.33) | copy-start | bytes 3538948
  304.8 4.6 copy-start.49
  304.8 4.6 copy-start.73
  304.8 7.4 copy-start.44
  337.1 5.6 copy-start.3
  337.1 10.2 copy-start.50
  342.7 6.0 copy-start.46
  342.7 6.0 copy-start.75
  347.3 13.4 %copy-start.23 = (f32[12,144,8]{1,2,0:T(8,128)}, f32[12,144,8]{1,2,0:T(8,128)S(1)}, u32[]{:S(2)}) copy-start(f32[12,144,8]{1,2,0:T(8,128)S(1)} %get-tuple-element.227) | copy-start | bytes 165892
  348.7 18.3 %copy-start.12 = (f32[12,144,384]{2,1,0:T(8,128)}, f32[12,144,384]{2,1,0:T(8,128)S(1)}, u32[]{:S(2)}) copy-start(f32[12,144,384]{2,1,0:T(8,128)S(1)} %convolution_add_fusion) | copy-start | bytes 7962628
  348.7 12.0 copy-start.8
  348.7 12.0 copy-start.33
  348.7 12.0 copy-start.52
  360.7 4.1 copy-start.77
  360.7 4.1 copy-start.36
  650.9 361.8 %reduce-scatter.3.cloned.1.call-start = ((), (), s32[]{:S(2)}) async-start(), calls=%async_computation.5 | async-start | bytes 13271040 | tf_op jit(solution)/shard_map/reduce_scatter | solution.py:223
  664.3 386.7 %all-reduce.7.cloned.1.call-start = ((), (), s32[]{:S(2)}) async-start(), calls=%async_computation.4 | async-start | bytes 294912 | tf_op jit(solution)/shard_map/psum | solution.py:177
  664.3 6.8 copy-start.19
  664.4 6.8 copy-start.31
  675.2 4.4 copy-start.13
  675.2 11.7 slice-start
  679.6 7.3 copy-start.9
  679.6 7.3 copy-start.34
  679.6 7.3 copy-start.37
  679.6 7.3 copy-start.53
  679.6 7.3 copy-start.66
  679.6 7.3 slice-start.1
  690.9 325.0 %copy-start.4 = (bf16[12,144,384]{2,1,0:T(8,128)(2,1)S(1)}, bf16[12,144,384]{2,1,0:T(8,128)(2,1)}, u32[]{:S(2)}) copy-start(bf16[12,144,384]{2,1,0:T(8,128)(2,1)} %param.22) | copy-start | bytes 3981316
  691.0 325.0 %copy-start.26 = (f32[12,144]{1,0:T(8,128)S(1)}, f32[12,144]{1,0:T(8,128)}, u32[]{:S(2)}) copy-start(f32[12,144]{1,0:T(8,128)} %copy-done.25) | copy-start | bytes 20740
  691.0 325.0 %copy-start.29 = (f32[12,144]{1,0:T(8,128)S(1)}, f32[12,144]{1,0:T(8,128)}, u32[]{:S(2)}) copy-start(f32[12,144]{1,0:T(8,128)} %copy-done.28) | copy-start | bytes 20740
  691.0 325.0 %copy-start.48 = (f32[384]{0:T(512)S(1)}, f32[384]{0:T(512)}, u32[]{:S(2)}) copy-start(f32[384]{0:T(512)} %copy-done.47) | copy-start | bytes 4612
  691.0 325.0 %copy-start.57 = (f32[384]{0:T(512)S(1)}, f32[384]{0:T(512)}, u32[]{:S(2)}) copy-start(f32[384]{0:T(512)} %copy-done.56) | copy-start | bytes 4612
  691.0 534.6 %all-reduce.9.cloned.1.call-start = ((), (), s32[]{:S(2)}) async-start(), calls=%async_computation.7 | async-start | bytes 14155776 | tf_op jit(solution)/shard_map/psum | solution.py:239
  1020.7 30.2 %copy-start.62 = (f32[12]{0:T(128)S(1)}, f32[12]{0:T(128)}, u32[]{:S(2)}) copy-start(f32[12]{0:T(128)} %get-tuple-element.197) | copy-start | bytes 148
  1020.7 31.9 %copy-start.22 = (bf16[384,1152]{1,0:T(8,128)(2,1)S(1)}, bf16[384,1152]{1,0:T(8,128)(2,1)}, u32[]{:S(2)}) copy-start(bf16[384,1152]{1,0:T(8,128)(2,1)} %param.25) | copy-start | bytes 2654212
  1052.6 4.6 copy-start.39
  1225.5 5.0 copy-start.16
  1225.5 6.4 copy-start.15
  1228.5 4.8 copy-start.1
  (26 other events, 57.6 us)
Sparse Core Ops, SparseCore 0:
  21.8 102.1 all-gather.5
  126.2 97.4 all-gather.3
  651.1 178.1 reduce-scatter.4
  831.6 181.1 reduce-scatter.2
  1015.5 35.3 all-reduce.6
  1059.3 166.2 all-reduce.8
where the time goes:
time: 1250 us; the launch traced here: 1240 us
  waiting for transfers between devices  623 us (50%)
  matrix products  357 us (29%)
  blocking collectives  83.1 us (7%)
  local copies, waits for them, and re-layouts  81.5 us (7%)
  other arithmetic  77 us (6%)
  between operations  18.5 us (1%)
    reduce_scatter x1, waiting for transfers between devices, per_device(): lax.psum_scatter(grad_key_all, 'seq', scatter_dimension=1, tiled=True)  180 us
    reduce_scatter x1, waiting for transfers between devices, per_device(): lax.psum_scatter(grad_value_all, 'seq', scatter_dimension=1, tiled=True)  138 us
    psum x1, waiting for transfers between devices, per_device(): lax.psum((grad_first_gain, grad_first_shift, grad_qkv_weight, grad_query_...  117 us
    dot_general x3, matrix products, attend_grad(): jnp.einsum('ghqk,gqhe->gkhe', grad_scores, queries, preferred_element_typ...  97.3 us
    dot_general x3, matrix products, attend_grad(): jnp.einsum('ghqk,gkhe->gqhe', grad_scores, keys_low, preferred_element_ty...  97.2 us
    all_gather x1, waiting for transfers between devices, per_device(): lax.all_gather(values, 'seq', axis=1, tiled=True)  90.9 us
    all_gather x1, waiting for transfers between devices, per_device(): lax.all_gather(keys_low, 'seq', axis=1, tiled=True)  71.8 us
    psum x1, blocking collectives, per_device(): lax.psum((grad_first_gain, grad_first_shift, grad_qkv_weight, grad_query_...  43.6 us
  transfers between devices with their start and end apart: 6, of which 6 were waited for; matrix products, arithmetic and copies ran while one was open for 7% of the time, Pallas kernels for 0%

commit v1 on v0

v1 whole, which is shorter than its diff:
```python
import jax
import jax.numpy as jnp
from jax import lax
from jax.experimental import pallas as pl
from jax.experimental.pallas import tpu as pltpu
from jax.sharding import PartitionSpec as P

f32, bf = jnp.float32, jnp.bfloat16
EPSILON = 1e-6
MASKED = -1e30
MIB = 1 << 20


def mm(a, b):
    return lax.dot_general(a, b, (((1,), (0,)), ((), ())), preferred_element_type=f32)


def mm_nt(a, b):
    return lax.dot_general(a, b, (((1,), (1,)), ((), ())), preferred_element_type=f32)


def mm_tn(a, b):
    return lax.dot_general(a, b, (((0,), (0,)), ((), ())), preferred_element_type=f32)


def row_mean(x):
    return jnp.sum(x, axis=-1, keepdims=True) * (1.0 / x.shape[-1])


def normalise(x):
    centred = x - row_mean(x)
    r = lax.rsqrt(row_mean(centred * centred) + EPSILON)
    return centred * r, r


def normal_parts(v):
    expo = jnp.exp(v * v * (-0.5))
    t = 1.0 / (1.0 + jnp.abs(v) * (0.3275911 * 0.7071067811865476))
    series = t * (0.127414796 + t * (-0.142248368 + t * (0.7107068705 + t * (-0.7265760135 + t * 0.5307027145))))
    tail = series * expo
    return jnp.where(v >= 0, 1.0 - tail, tail), expo * 0.3989422804014327


def split2(a):
    high = a.astype(bf)
    return high, (a - high.astype(f32)).astype(bf)


def attend_kernel(parts, rows, slot, *refs):
    x_refs, flag_refs = refs[:parts], refs[parts:2 * parts]
    vec_ref, wqkv, wout = refs[2 * parts:2 * parts + 3]
    qa_ref, k_ref, v_ref, caug_ref, att_ref, mid_ref = refs[2 * parts + 3:2 * parts + 9]
    nrm_s, q_s = refs[2 * parts + 9:]
    n, width = nrm_s.shape
    vec = lambda i: vec_ref[i:i + 1, :]
    r8 = lax.broadcasted_iota(jnp.int32, (8, 128), 0)
    l8 = lax.broadcasted_iota(jnp.int32, (8, 128), 1) & 63
    place = ((r8 == 0) & (l8 == 3)) | ((r8 == 1) & (l8 < 3)) | ((r8 == 2) & (l8 == 4))
    place = jnp.where(place, 1.0, 0.0).astype(bf)
    row = lax.broadcasted_iota(jnp.int32, (8, rows), 0)
    for i in range(parts):
        rs = slice(i * rows, (i + 1) * rows)
        xh, _ = normalise(x_refs[i][0:rows, :].astype(f32))
        nrm_s[rs, :] = (xh * vec(0) + vec(1)).astype(bf)
        keep = flag_refs[i][rows:rows + 16, 0:rows].astype(f32)[slot:slot + 1, :]
        marks = jnp.where(row == 0, (1.0 - keep) * MASKED, jnp.where(row == 1, 1.0, jnp.where(row == 2, keep, 0.0)))
        caug_ref[rs, :] = mm_tn(marks.astype(bf), place).astype(bf)
    nrm = nrm_s[...]
    q_s[...] = (mm(nrm, wqkv[:, 0:width]) + vec(2)).astype(bf) * jnp.asarray(0.125, bf)
    k_ref[...] = mm(nrm, wqkv[:, width:2 * width]).astype(bf)
    v_ref[...] = (mm(nrm, wqkv[:, 2 * width:3 * width]) + vec(3)).astype(bf)
    lane = lax.broadcasted_iota(jnp.int32, (n, 128), 1)
    lane64 = lane & 63
    ones = jnp.ones((n, 128), bf)
    for j in range(width // 128):
        sl = slice(128 * j, 128 * j + 128)
        outs = []
        for e in range(2):
            own = (lane < 64) if e == 0 else (lane >= 64)
            kp = jnp.where(own, k_ref[:, sl], caug_ref[...])
            qp = jnp.where(own, q_s[:, sl], jnp.where(lane64 == 3, 1.0, 0.0).astype(bf))
            s = mm_nt(qp, kp)
            m = jnp.max(s, axis=-1, keepdims=True)
            p = jnp.exp(s - m).astype(bf)
            o = mm(p, jnp.concatenate([v_ref[:, sl], ones], axis=1))
            total = o[:, 128:256]
            outs.append(o[:, 0:128] / total)
            logs = -(m + jnp.log(total))
            hi = logs.astype(bf).astype(f32)
            lo = (logs - hi).astype(bf).astype(f32)
            aug = jnp.where(lane64 == 0, hi, jnp.where(lane64 == 1, lo, jnp.where(lane64 == 2, logs - hi - lo, jnp.where(lane64 == 3, 1.0, 0.0))))
            h = 2 * j + e
            qa_ref[:, 128 * h:128 * h + 128] = jnp.where(own, q_s[:, sl], aug.astype(bf))
        att_ref[:, sl] = jnp.where(lane < 64, outs[0], outs[1]).astype(bf)
    pr = mm(att_ref[...], wout[...])
    for i in range(parts):
        rs = slice(i * rows, (i + 1) * rows)
        mid_ref[rs, :] = x_refs[i][0:rows, :].astype(f32) + pr[rs, :] + vec(4)


def attend_call(pieces, flags, slot, rows, vec, wqkv, wout):
    parts, width = len(pieces), wout.shape[0]
    n = parts * rows
    vm = pl.BlockSpec(memory_space=pltpu.VMEM)
    outs = [((n, 2 * width), bf), ((n, width), bf), ((n, width), bf), ((n, 128), bf), ((n, width), bf), ((n, width), f32)]
    return pl.pallas_call(
        lambda *refs: attend_kernel(parts, rows, slot, *refs),
        out_shape=[jax.ShapeDtypeStruct(s, d) for s, d in outs],
        in_specs=[vm] * (2 * parts + 3), out_specs=[vm] * 6,
        scratch_shapes=[pltpu.VMEM((n, width), bf), pltpu.VMEM((n, width), bf)],
        compiler_params=pltpu.CompilerParams(vmem_limit_bytes=VM_A * MIB),
        cost_estimate=pl.CostEstimate(flops=7_000_000_000, bytes_accessed=1_000_000, transcendentals=2_000_000),
        name="attend",
    )(*pieces, *flags, vec, wqkv, wout)


def feed_kernel(slot, own_count, first, *refs):
    mid_ref, att_ref, caug_ref, vec_ref, mb_ref, mapw_ref, cot_ref, valid_ref, count_ref, wout, wup, wdn = refs[:12]
    refs = refs[12:]
    if first:
        acc_in = sm_in = None
    else:
        acc_in, sm_in = refs[:2]
        refs = refs[2:]
    gm_ref, doa_ref, learn_ref, acc, sm = refs[:5]
    sec_s, hid_s, gp_s, g_s = refs[5:]
    n, width = mid_ref.shape
    blocks = hid_s.shape[1] // width
    tokens = mapw_ref.shape[0]
    vec = lambda i: vec_ref[i:i + 1, :]
    place = lax.axis_index("seq") * own_count + slot

    def add(ref, ref_in, rows, value):
        ref[rows, :] = value if first else ref_in[rows, :] + value

    xh, _ = normalise(mid_ref[...])
    sec_s[...] = (xh * vec(5) + vec(6)).astype(bf)
    total = None
    for j in range(blocks):
        js = slice(width * j, width * (j + 1))
        pre = mm(sec_s[...], wup[:, js]) + vec(8 + j)
        upper, density = normal_parts(pre)
        hid_s[:, js] = (pre * upper).astype(bf)
        gp_s[:, js] = upper + pre * density
        t = mm(hid_s[:, js], wdn[js, :])
        total = t if total is None else total + t
    out = mid_ref[...] + total + vec(7)
    ohi, olo = split2(out)
    cm = jnp.concatenate([mapw_ref[...].astype(f32), cot_ref[place].astype(f32)], axis=0).astype(bf)
    lg = mm_nt(cm, ohi) + mm_nt(cm, olo)
    pick = jnp.where(lax.broadcasted_iota(jnp.int32, (8, 128), 1) == 4, 1.0, 0.0).astype(bf)
    keep = mm_nt(pick, caug_ref[...])[0:1, :]
    maps = jax.nn.sigmoid(lg[0:tokens, :] + mb_ref[:, 0:1])
    inverse = 1.0 / jnp.sum(keep, axis=-1, keepdims=True)
    tot = jnp.sum(maps, axis=0, keepdims=True)
    inter = jnp.sum(keep * (tot * tot - jnp.sum(maps * maps, axis=0, keepdims=True)), axis=-1, keepdims=True)
    valid = valid_ref[place].astype(f32)
    gmaps = keep * (lg[tokens:2 * tokens, :] * inverse + (2.0 * valid / count_ref[0:1, 0:1]) * (tot - maps))
    gl = gmaps * maps * (1.0 - maps)
    mk = maps * keep
    mkh, mkl = split2(mk)
    glh, gll = split2(gl)
    st = jnp.concatenate([mkh.astype(f32), mkl.astype(f32), glh.astype(f32), gll.astype(f32)], axis=0).astype(bf)
    r1 = mm(st, ohi) + mm(st, olo)
    learn_ref[...] = (r1[0:tokens, :] + r1[tokens:2 * tokens, :]) * inverse
    add(sm, sm_in, slice(8, 16), r1[2 * tokens:3 * tokens, :] + r1[3 * tokens:, :])
    gah, gal = split2(mk * inverse)
    lhs = jnp.concatenate([glh.astype(f32), gah.astype(f32), gll.astype(f32), gal.astype(f32)], axis=0).astype(bf)
    g = mm_tn(lhs, jnp.concatenate([cm, cm], axis=0))
    g_s[...] = g
    add(sm, sm_in, slice(0, 1), jnp.sum(g, axis=0, keepdims=True))
    glow = g.astype(bf)
    g_t = glow.T
    sec_t = sec_s[...].T
    gsec = None
    for j in range(blocks):
        js = slice(width * j, width * (j + 1))
        gh = mm_nt(glow, wdn[js, :]).astype(bf).astype(f32)
        gpre = gh * gp_s[:, js]
        gpl = gpre.astype(bf)
        add(sm, sm_in, slice(4 + j, 5 + j), jnp.sum(gpre, axis=0, keepdims=True))
        t = mm_nt(gpl, wup[:, js])
        gsec = t if gsec is None else gsec + t
        add(acc, acc_in, js, mm(g_t, hid_s[:, js]))
        add(acc, acc_in, slice(width * (blocks + j), width * (blocks + j + 1)), mm(sec_t, gpl))
    xh, r = normalise(mid_ref[...])
    gg = gsec * vec(5)
    gm = g_s[...] + r * (gg - row_mean(gg) - xh * row_mean(gg * xh))
    gm_ref[...] = gm
    gml = gm.astype(bf)
    add(sm, sm_in, slice(1, 2), jnp.sum(gm, axis=0, keepdims=True))
    add(sm, sm_in, slice(2, 3), jnp.sum(gsec * xh, axis=0, keepdims=True))
    add(sm, sm_in, slice(3, 4), jnp.sum(gsec, axis=0, keepdims=True))
    glb = jnp.sum(gl, axis=-1, keepdims=True)
    lr = lax.broadcasted_iota(jnp.int32, (8, width), 1)
    rr = lax.broadcasted_iota(jnp.int32, (8, width), 0)
    add(sm, sm_in, slice(16, 24), jnp.where(lr == 0, glb, jnp.where((lr == 1) & (rr == 0), valid * inter * (1.0 / n), 0.0)))
    used = width * (2 * blocks + 1)
    add(acc, acc_in, slice(2 * blocks * width, used), mm(att_ref[...].T, gml))
    if first and acc.shape[0] > used:
        acc[used:, :] = jnp.zeros((acc.shape[0] - used, width), f32)
    do = mm_nt(gml, wout[...]).astype(bf).astype(f32)
    lane = lax.broadcasted_iota(jnp.int32, (n, 128), 1)
    lane64 = lane & 63
    for j in range(width // 128):
        sl = slice(128 * j, 128 * j + 128)
        dj = do[:, sl]
        pd = dj * att_ref[:, sl].astype(f32)
        for e in range(2):
            own = (lane < 64) if e == 0 else (lane >= 64)
            dl = -jnp.sum(jnp.where(own, pd, 0.0), axis=-1, keepdims=True)
            hi = dl.astype(bf).astype(f32)
            aug = jnp.where(lane64 == 0, hi, jnp.where(lane64 == 1, dl - hi, 0.0))
            h = 2 * j + e
            doa_ref[:, 128 * h:128 * h + 128] = jnp.where(own, dj, aug).astype(bf)


def feed_call(slot, own_count, packed_rows, mid, att, caug, vec, mb, mapw, cot, valid, count, wout, wup, wdn, acc, sm):
    n, width = mid.shape
    hidden = wup.shape[1]
    first = acc is None
    vm = pl.BlockSpec(memory_space=pltpu.VMEM)
    smem = pl.BlockSpec(memory_space=pltpu.SMEM)
    outs = [((n, width), f32), ((n, 2 * width), bf), ((8, width), f32), ((packed_rows, width), f32), ((24, width), f32)]
    args = (mid, att, caug, vec, mb, mapw, cot, valid, count, wout, wup, wdn)
    extra = () if first else (acc, sm)
    return pl.pallas_call(
        lambda *refs: feed_kernel(slot, own_count, first, *refs),
        out_shape=[jax.ShapeDtypeStruct(s, d) for s, d in outs],
        in_specs=[vm] * 7 + [smem] + [vm] * (4 + len(extra)), out_specs=[vm] * 5,
        input_output_aliases={} if first else {12: 3, 13: 4},
        scratch_shapes=[pltpu.VMEM((n, width), bf), pltpu.VMEM((n, hidden), bf), pltpu.VMEM((n, hidden), f32), pltpu.VMEM((n, width), f32)],
        compiler_params=pltpu.CompilerParams(vmem_limit_bytes=VM_F * MIB),
        cost_estimate=pl.CostEstimate(flops=13_000_000_000, bytes_accessed=1_000_000, transcendentals=2_000_000),
        name="feed",
    )(*args, *extra)


def back_kernel(parts, rows, first, *refs):
    x_refs = refs[:parts]
    qa, k_ref, v_ref, doa, caug, gm, vec_ref, wqkv = refs[parts:parts + 8]
    refs = refs[parts + 8:]
    if first:
        dwq_in = sm_in = None
    else:
        dwq_in, sm_in = refs[:2]
        refs = refs[2:]
    g_refs, (dwq, sm, dm_s) = refs[:parts], refs[parts:]
    n, width = k_ref.shape
    step = n // 3 if n % 48 == 0 else n
    vec = lambda i: vec_ref[i:i + 1, :]

    def add(ref, ref_in, at, value):
        ref[at] = value if first else ref_in[at] + value

    k_t = k_ref[...].T
    lane = lax.broadcasted_iota(jnp.int32, (step, 128), 1)
    ones = jnp.ones((step, 128), bf)
    for j in range(width // 128):
        sl = slice(128 * j, 128 * j + 128)
        dqt = [None, None]
        dvsum = None
        for c in range(n // step):
            cs = slice(c * step, c * step + step)
            dvs, dks = [], []
            for e in range(2):
                h = 2 * j + e
                hs = slice(128 * h, 128 * h + 128)
                own = (lane < 64) if e == 0 else (lane >= 64)
                kp = jnp.where(own, k_ref[cs, sl], caug[cs, :])
                vp = jnp.where(own, v_ref[cs, sl], ones)
                p = jnp.exp(mm_nt(kp, qa[:, hs]))
                ds = (p * mm_nt(vp, doa[:, hs])).astype(bf)
                dvs.append(mm(p.astype(bf), doa[:, hs]))
                dks.append(mm(ds, qa[:, hs]))
                t = mm(k_t[64 * h:64 * h + 64, cs], ds)
                dqt[e] = t if dqt[e] is None else dqt[e] + t
            dm_s[cs, width + 128 * j:width + 128 * j + 128] = jnp.where(lane < 64, dks[0], dks[1]).astype(bf)
            dv = jnp.where(lane < 64, dvs[0], dvs[1])
            dm_s[cs, 2 * width + 128 * j:2 * width + 128 * j + 128] = dv.astype(bf)
            s = jnp.sum(dv, axis=0, keepdims=True)
            dvsum = s if dvsum is None else dvsum + s
        add(sm, sm_in, (slice(3, 4), sl), dvsum)
        dq = jnp.concatenate(dqt, axis=0).T * 0.125
        add(sm, sm_in, (slice(2, 3), sl), jnp.sum(dq, axis=0, keepdims=True))
        dm_s[:, sl] = dq.astype(bf)
    x = jnp.concatenate([ref[0:rows, :] for ref in x_refs], axis=0).astype(f32)
    xh, r = normalise(x)
    nrm_t = (xh * vec(0) + vec(1)).astype(bf).T
    for j in range(3):
        js = slice(width * j, width * (j + 1))
        add(dwq, dwq_in, (js, slice(None)), mm(nrm_t, dm_s[:, js]))
    if first:
        if dwq.shape[0] > 3 * width:
            dwq[3 * width:, :] = jnp.zeros((dwq.shape[0] - 3 * width, width), f32)
        sm[4:8, :] = jnp.zeros((4, width), f32)
    else:
        sm[4:8, :] = sm_in[4:8, :]
    gf = mm_nt(dm_s[...], wqkv[...])
    gg = gf * vec(0)
    gx = gm[...] + r * (gg - row_mean(gg) - xh * row_mean(gg * xh))
    add(sm, sm_in, (slice(0, 1), slice(None)), jnp.sum(gf * xh, axis=0, keepdims=True))
    add(sm, sm_in, (slice(1, 2), slice(None)), jnp.sum(gf, axis=0, keepdims=True))
    for i in range(parts):
        g_refs[i][...] = gx[i * rows:(i + 1) * rows, :].astype(bf)


def back_call(pieces, rows, packed_rows, qa, k, v, doa, caug, gm, vec, wqkv, dwq, sm):
    parts = len(pieces)
    n, width = k.shape
    first = dwq is None
    vm = pl.BlockSpec(memory_space=pltpu.VMEM)
    outs = [((rows, width), bf)] * parts + [((packed_rows, width), f32), ((8, width), f32)]
    extra = () if first else (dwq, sm)
    base = parts + 8
    return pl.pallas_call(
        lambda *refs: back_kernel(parts, rows, first, *refs),
        out_shape=[jax.ShapeDtypeStruct(s, d) for s, d in outs],
        in_specs=[vm] * (base + len(extra)), out_specs=[vm] * (parts + 2),
        input_output_aliases={} if first else {base: parts, base + 1: parts + 1},
        scratch_shapes=[pltpu.VMEM((n, 3 * width), bf)],
        compiler_params=pltpu.CompilerParams(vmem_limit_bytes=VM_B * MIB),
        cost_estimate=pl.CostEstimate(flops=8_000_000_000, bytes_accessed=1_000_000, transcendentals=2_000_000),
        name="back",
    )(*pieces, qa, k, v, doa, caug, gm, vec, wqkv, *extra)


def unpack_kernel(hidden, a0, a1, b0, b1, gdn, gup, gout, gqkv, a_s, b_s):
    side = lax.axis_index("dp") & 1
    half_a, width = a0.shape
    half_b = b0.shape[0]
    a_s[pl.ds(pl.multiple_of(side * half_a, 16), half_a), :] = a0[...]
    a_s[pl.ds(pl.multiple_of((1 - side) * half_a, 16), half_a), :] = a1[...]
    b_s[pl.ds(pl.multiple_of(side * half_b, 16), half_b), :] = b0[...]
    b_s[pl.ds(pl.multiple_of((1 - side) * half_b, 16), half_b), :] = b1[...]
    blocks = hidden // width
    for j in range(blocks):
        js = slice(width * j, width * (j + 1))
        gdn[js, :] = a_s[js, :].T.astype(f32)
        gup[:, js] = a_s[width * (blocks + j):width * (blocks + j + 1), :].astype(f32)
    gout[...] = a_s[2 * blocks * width:(2 * blocks + 1) * width, :].astype(f32)
    for j in range(3):
        js = slice(width * j, width * (j + 1))
        gqkv[:, js] = b_s[js, :].astype(f32)


def unpack_call(hidden, a0, a1, b0, b1):
    width = a0.shape[1]
    vm = pl.BlockSpec(memory_space=pltpu.VMEM)
    outs = [(hidden, width), (width, hidden), (width, width), (width, 3 * width)]
    return pl.pallas_call(
        lambda *refs: unpack_kernel(hidden, *refs),
        out_shape=[jax.ShapeDtypeStruct(s, f32) for s in outs],
        in_specs=[vm] * 4, out_specs=[vm] * 4,
        scratch_shapes=[pltpu.VMEM((2 * a0.shape[0], width), bf), pltpu.VMEM((2 * b0.shape[0], width), bf)],
        compiler_params=pltpu.CompilerParams(vmem_limit_bytes=24 * MIB),
        name="unpack",
    )(a0, a1, b0, b1)


def place_kernel(parts, own, *refs):
    out = refs[parts * own]
    me = lax.axis_index("seq")
    for k in range(parts):
        for i in range(own):
            out[(me ^ k) * own + i] = refs[i * parts + k][...].astype(f32)


def place_call(got):
    own, parts = len(got), len(got[0])
    rows, width = got[0][0].shape
    vm = pl.BlockSpec(memory_space=pltpu.VMEM)
    return pl.pallas_call(
        lambda *refs: place_kernel(parts, own, *refs),
        out_shape=jax.ShapeDtypeStruct((parts * own, rows, width), f32),
        in_specs=[vm] * (parts * own), out_specs=vm,
        compiler_params=pltpu.CompilerParams(vmem_limit_bytes=8 * MIB),
        name="place",
    )(*[g for image in got for g in image])


VM_A, VM_F, VM_B = 24, 32, 24


def xor_permute(x, axis, k):
    return lax.ppermute(x, axis, [(i, i ^ k) for i in range(lax.axis_size(axis))])


def after(x, *others):
    return lax.optimization_barrier((x,) + others)[0]


def tree_sum(parts):
    while len(parts) > 1:
        parts = [parts[i] + parts[i + 1] for i in range(0, len(parts), 2)]
    return parts[0]


def pick(x, index):
    return lax.dynamic_index_in_dim(x, index, 0, keepdims=False)


def halves(small):
    high = lax.reduce_precision(small, 8, 7)
    return jnp.concatenate([high, lax.reduce_precision(small - high, 8, 7)], axis=0).astype(bf)


def whole(pair):
    rows = pair.shape[0] // 2
    return pair[:rows].astype(f32) + pair[rows:].astype(f32)


def scatter_stage(big, small, axis, index, count, shift):
    chunks = big.reshape(count, big.shape[0] // count, big.shape[1])
    rows = chunks.shape[1]
    pair = halves(small)
    kept = [pick(chunks, index).astype(f32)]
    smalls = [whole(pair)]
    for k in range(1, count):
        sent = jnp.concatenate([pick(chunks, index ^ k).astype(bf), pair], axis=0)
        got = xor_permute(sent, axis, k << shift)
        kept.append(got[:rows].astype(f32))
        smalls.append(whole(got[rows:]))
    return tree_sum(kept), tree_sum(smalls)


def gather_stage(part, axis, index, count, shift):
    out = jnp.zeros((count,) + part.shape, part.dtype)
    out = lax.dynamic_update_index_in_dim(out, part, index, 0)
    for k in range(1, count):
        got = xor_permute(part, axis, k << shift)
        out = lax.dynamic_update_index_in_dim(out, got, index ^ k, 0)
    return out


class Reduction:
    def __init__(self):
        self.dp, self.seq = lax.axis_index("dp"), lax.axis_index("seq")
        self.chips, self.depth = lax.axis_size("dp") // 2, lax.axis_size("seq")

    def core(self, big, small):
        return scatter_stage(big, small, "dp", self.dp & 1, 2, 0)

    def plane(self, big, small):
        return scatter_stage(big, small, "dp", self.dp >> 1, self.chips, 1)

    def column(self, big, small):
        return scatter_stage(big, small, "seq", self.seq, self.depth, 0)

    def spread_column(self, part, rider=None):
        part = part.astype(bf)
        rows, width = part.shape
        if rider is not None:
            part = jnp.concatenate([part, rider], axis=0)
        part = gather_stage(part, "seq", self.seq, self.depth, 0)
        return part[:, :rows].reshape(-1, width), part[:, rows:]

    def spread_plane(self, part):
        return gather_stage(part, "dp", self.dp >> 1, self.chips, 1).reshape(-1, part.shape[1])

    def spread_core(self, part):
        return part, xor_permute(part, "dp", 1)


def padded(rows, unit):
    return rows + -rows % unit


def per_device(
    patches, first_gain, first_shift, qkv_weight, query_value_bias, out_weight, out_bias,
    second_gain, second_shift, up_weight, up_bias, down_weight, down_bias, map_weight, map_bias,
    keep_mask, image_valid, token_cotangent,
):
    images, rows, width = patches.shape
    me = lax.axis_index("seq")
    depth, dps = lax.axis_size("seq"), lax.axis_size("dp")
    own = images // depth
    hidden, tokens = up_weight.shape[1], map_weight.shape[1]
    nb = hidden // width
    unit = 8 * dps * depth
    rows_a, rows_b = padded((2 * nb + 1) * width, unit), padded(3 * width, unit)

    blocks = patches.reshape(depth, own, rows, width)
    flags = keep_mask.astype(bf).reshape(depth, own, rows)
    flags = jnp.pad(flags, ((0, 0), (0, 16 - own), (0, width - rows)))
    order = sorted(range(1, depth), key=lambda k: (k == 1, k))
    pieces = []
    hold = None
    for i in range(own):
        got = [None] * depth
        for k in [0] + order:
            b = pick(blocks, me ^ k)[i]
            if i == 0:
                b = jnp.concatenate([b, pick(flags, me ^ k)], axis=0)
            if k > 0:
                if hold is not None:
                    b = after(b, hold)
                b = xor_permute(b, "seq", k)
            got[k] = b
        hold = got[order[-1]]
        pieces.append(got)

    count = jnp.broadcast_to(jnp.sum(image_valid.astype(f32)), (8, 128))
    step = 1
    while step < dps:
        count = count + xor_permute(count, "dp", step)
        step *= 2
    vec = jnp.concatenate([
        first_gain, first_shift, query_value_bias, out_bias, second_gain, second_shift, down_bias,
        up_bias, jnp.zeros((4 * width,), bf),
    ]).astype(f32).reshape(-1, width)
    mb = jnp.broadcast_to(map_bias.astype(f32)[:, None], (tokens, 128))
    mapw = map_weight.T

    saved, learned = [], []
    acc = sm = tok = None
    for i in range(own):
        v = vec if tok is None else after(vec, tok)
        qa, key, val, caug, att, mid = attend_call(pieces[i], pieces[0], i, rows, v, qkv_weight, out_weight)
        gm, doa, learn, acc, sm = feed_call(
            i, own, rows_a, mid, att, caug, vec, mb, mapw, token_cotangent, image_valid, count,
            out_weight, up_weight, down_weight, acc, sm)
        tok = sm
        saved.append((qa, key, val, doa, caug, gm))
        learned.append(learn)
    red = Reduction()
    rider = halves(jnp.concatenate(learned, axis=0))
    big, small = red.core(acc, sm)

    dwq = smq = None
    sent = []
    for i in range(own):
        if i == 0:
            v = after(vec, tok)
        elif i == 1:
            v = after(vec, smq, small)
            big, small = red.plane(big, small)
        else:
            v = after(vec, smq, small)
        if i == own - 1:
            big, small = red.column(big, small)
        o = back_call(pieces[i], rows, rows_b, *saved[i], v, qkv_weight, dwq, smq)
        dwq, smq = o[depth], o[depth + 1]
        sent.append(o[:depth])
    got = [[g if k == 0 else xor_permute(g, "seq", k) for k, g in enumerate(s)] for s in sent]
    part, rider = red.spread_column(big, rider)
    part = red.spread_plane(part)
    a0, a1 = red.spread_core(part)
    bigb, smallb = red.core(dwq, smq)
    bigb, smallb = red.plane(bigb, smallb)
    bigb, smallb = red.column(bigb, smallb)
    partb, _ = red.spread_column(bigb)
    partb = red.spread_plane(partb)
    b0, b1 = red.spread_core(partb)
    gdn, gup, gout, gqkv = unpack_call(hidden, a0, a1, b0, b1)
    outs = place_call(got)

    n = own * tokens
    learned = (rider[:, :n].astype(f32) + rider[:, n:].astype(f32)).reshape(images, tokens, width)
    penalty = small[16, 1] / count[0, 0]
    return (
        learned, penalty, outs, smallb[0], smallb[1], gqkv, smallb[2:4].reshape(-1), gout, small[1],
        small[2], small[3], gup, small[4:4 + nb].reshape(-1), gdn, small[0],
        small[8:16].T, small[16:24, 0],
    )


def solution(mesh):
    rep = P()
    placed = (P("dp", "seq", None),) + (rep,) * 14 + (P("dp", "seq"), P("dp"), P("dp", None, None))
    return jax.shard_map(
        per_device, mesh=mesh, in_specs=placed,
        out_specs=(P("dp", None, None), rep, P("dp", "seq", None)) + (rep,) * 14,
        check_vma=False,
    )
```

time: 1250 us -> 249 us (0.20)
  waiting for transfers between devices: 623 us -> 55.5 us
  matrix products: 357 us -> 0 us
  Pallas kernels: 0 us -> 86.1 us
  blocking collectives: 83.1 us -> 0 us
  other arithmetic: 77 us -> 9.51 us
  starting transfers between devices: 0.42 us -> 65.9 us
  local copies, waits for them, and re-layouts: 81.5 us -> 24 us
  between operations: 18.5 us -> 4.49 us
    dot_general x39 -> x0, matrix products: 357 us -> none  [the longest x3 97.3 us: attend_grad(): jnp.einsum('ghqk,gqhe->gkhe', grad_scores, queries, preferred_element_typ...]
    reduce_scatter x2 -> x0, waiting for transfers between devices: 318 us -> none  [the longest x1 180 us: per_device(): lax.psum_scatter(grad_key_all, 'seq', scatter_dimension=1, tiled=True)]
    all_gather x2 -> x0, waiting for transfers between devices: 163 us -> none  [the longest x1 90.9 us: per_device(): lax.all_gather(values, 'seq', axis=1, tiled=True)]
    psum x2 -> x0, waiting for transfers between devices: 143 us -> none  [the longest x1 117 us: per_device(): lax.psum((grad_first_gain, grad_first_shift, grad_qkv_weight, grad_query_...]
    pallas_call x0 -> x11, Pallas kernels: none -> 86.1 us  [the longest x3 37.5 us: feed_call(): pl.pallas_call(lambda *refs: feed_kernel(slot, own_count, first, *refs),...]
    psum x3 -> x0, blocking collectives: 65.9 us -> none  [the longest x1 43.6 us: per_device(): lax.psum((grad_first_gain, grad_first_shift, grad_qkv_weight, grad_query_...]
    ppermute x0 -> x49, starting transfers between devices: none -> 65.9 us  [xor_permute(): lax.ppermute(x, axis, [(i, i ^ k) for i in range(lax.axis_size(axis))])]
    ppermute x0 -> x49, waiting for transfers between devices: none -> 55.5 us  [xor_permute(): lax.ppermute(x, axis, [(i, i ^ k) for i in range(lax.axis_size(axis))])]
  transfers between devices with their start and end apart: 6 -> 49, of which waited for: 6 -> 17; matrix products, arithmetic and copies ran while one was open for 7% -> 7% of each run, Pallas kernels for 0% -> 26%
where the time goes in v1:
time: 249 us; the launch traced here: 245 us
  Pallas kernels  86.1 us (35%)
  starting transfers between devices  65.9 us (26%)
  waiting for transfers between devices  55.5 us (22%)
  local copies, waits for them, and re-layouts  24 us (10%)
  other arithmetic  9.51 us (4%)
  between operations  4.49 us (2%)
    ppermute x49, starting transfers between devices, xor_permute(): lax.ppermute(x, axis, [(i, i ^ k) for i in range(lax.axis_size(axis))])  65.9 us
    ppermute x49, waiting for transfers between devices, xor_permute(): lax.ppermute(x, axis, [(i, i ^ k) for i in range(lax.axis_size(axis))])  55.5 us
    pallas_call x3, Pallas kernels, feed_call(): pl.pallas_call(lambda *refs: feed_kernel(slot, own_count, first, *refs),...  37.5 us
    pallas_call x3, Pallas kernels, back_call(): pl.pallas_call(lambda *refs: back_kernel(parts, rows, first, *refs), out_...  26.4 us
    pallas_call x3, Pallas kernels, attend_call(): pl.pallas_call(lambda *refs: attend_kernel(parts, rows, slot, *refs), out...  15.7 us
    unnamed x124, local copies, waits for them, and re-layouts  14.6 us
  transfers between devices with their start and end apart: 49, of which 17 were waited for; matrix products, arithmetic and copies ran while one was open for 7% of the time, Pallas kernels for 26%

profile of v1, /device:TPU:0, one launch (start us, length us, event | category | flops | bytes accessed | tf_op | source)
XLA Modules:
  0.0 245.5 jit_solution(15498198796328721676)
XLA Ops:
  1.6 2.3 dynamic-slice_bitcast_fusion.6
  3.9 3.1 %collective-permute-start = (bf16[160,384]{1,0:T(8,128)(2,1)S(1)}, bf16[160,384]{1,0:T(8,128)(2,1)S(1)}, u32[]{:S(2)}, u32[]{:S(2)}) collective-permute-start(bf16[160,384]{1,0:T(8,128)(2,1)S(1)} %pad_maximum_fusion.20), channel_id=1, source_target_pairs={{0,1},{1,0},{2,3},{3,2},{4,5},{5,4},{6,7},{7,6},{8,9},{9,8},{10,11... | collective-permute-start | bytes 368648 | tf_op jit(solution)/shard_map/ppermute | solution.py:386
  8.4 2.7 %collective-permute-start.5 = (bf16[160,384]{1,0:T(8,128)(2,1)S(1)}, bf16[160,384]{1,0:T(8,128)(2,1)S(1)}, u32[]{:S(2)}, u32[]{:S(2)}) collective-permute-start(bf16[160,384]{1,0:T(8,128)(2,1)S(1)} %pad_maximum_fusion.22), channel_id=1, source_target_pairs={{0,2},{1,3},{2,0},{3,1},{4,6},{5,7},{6,4},{7,5},{8,10},{9,11},{10,... | collective-permute-start | bytes 368648 | tf_op jit(solution)/shard_map/ppermute | solution.py:386
  11.7 1.6 collective-permute-start.10
  13.2 1.0 collective-permute-start.6
  14.3 1.1 collective-permute-done.10
  16.0 1.6 collective-permute-start.11
  20.4 1.9 collective-permute-start.7
  22.4 2.1 collective-permute-start.8
  24.5 5.2 %attend.3 = (bf16[576,768]{1,0:T(8,128)(2,1)S(1)}, bf16[576,384]{1,0:T(8,128)(2,1)S(1)}, bf16[576,384]{1,0:T(8,128)(2,1)S(1)}, bf16[576,128]{1,0:T(8,128)(2,1)S(...) custom-call(bf16[160,384]{1,0:T(8,128)(2,1)S(1)} %pad_maximum_fusion.21.refs_0_.refs_4_, ...), custom_call_target="tpu_custom_call" | custom-call | flops 7000000000 | bytes 1000000 | tf_op jit(solution)/shard_map/attend/pallas_call | solution.py:106
  31.3 12.1 %feed.3 = (f32[576,384]{1,0:T(8,128)S(1)}, bf16[576,768]{1,0:T(8,128)(2,1)S(1)}, f32[8,384]{1,0:T(8,128)S(1)}, f32[3584,384]{1,0:T(8,128)S(1)}, f32[24,384]{1,0:T(8,128)S(1)}) custom-call(f32[576,384]{1,0:T(8,128)S(1)} %get-tuple-element.89.refs_0_, bf16[576,384]{1,0:T(8,128)(2,1)S(1)} %get-tuple-element.90.refs_1_, ...), custom_call_target="tpu_custom_call" | custom-call | flops 12999999488 | bytes 1000000 | tf_op jit(solution)/shard_map/feed/pallas_call | solution.py:227
  43.5 2.4 collective-permute-start.3
  45.9 2.0 collective-permute-start.4
  47.9 5.2 %attend.4 = (bf16[576,768]{1,0:T(8,128)(2,1)S(1)}, bf16[576,384]{1,0:T(8,128)(2,1)S(1)}, bf16[576,384]{1,0:T(8,128)(2,1)S(1)}, bf16[576,128]{1,0:T(8,128)(2,1)S(...) custom-call(bf16[144,384]{1,0:T(8,128)(2,1)S(1)} %get-tuple-element.177.refs_0_, ...), custom_call_target="tpu_custom_call" | custom-call | flops 7000000000 | bytes 1000000 | tf_op jit(solution)/shard_map/attend/pallas_call | solution.py:106
  53.2 12.9 %feed.4 = (f32[576,384]{1,0:T(8,128)S(1)}, bf16[576,768]{1,0:T(8,128)(2,1)S(1)}, f32[8,384]{1,0:T(8,128)S(1)}, f32[3584,384]{1,0:T(8,128)S(1)}, f32[24,384]{1,0:T(8,128)S(1)}) custom-call(f32[576,384]{1,0:T(8,128)S(1)} %get-tuple-element.94.refs_0_, bf16[576,384]{1,0:T(8,128)(2,1)S(1)} %get-tuple-element.95.refs_1_, ...), custom_call_target="tpu_custom_call", output_to_operand_aliasing={{3}: (12, {}), {4}: (13, {})} | custom-call | flops 12999999488 | bytes 1000000 | tf_op jit(solution)/shard_map/feed/pallas_call | solution.py:227
  66.2 5.3 %attend.5 = (bf16[576,768]{1,0:T(8,128)(2,1)S(1)}, bf16[576,384]{1,0:T(8,128)(2,1)S(1)}, bf16[576,384]{1,0:T(8,128)(2,1)S(1)}, bf16[576,128]{1,0:T(8,128)(2,1)S(...) custom-call(bf16[144,384]{1,0:T(8,128)(2,1)S(1)} %get-tuple-element.173.refs_0_, ...), custom_call_target="tpu_custom_call" | custom-call | flops 7000000000 | bytes 1000000 | tf_op jit(solution)/shard_map/attend/pallas_call | solution.py:106
  73.1 12.5 %feed.5 = (f32[576,384]{1,0:T(8,128)S(1)}, bf16[576,768]{1,0:T(8,128)(2,1)S(1)}, f32[8,384]{1,0:T(8,128)S(1)}, f32[3584,384]{1,0:T(8,128)S(1)}, f32[24,384]{1,0:T(8,128)S(1)}) custom-call(f32[576,384]{1,0:T(8,128)S(1)} %get-tuple-element.100.refs_0_, ...), custom_call_target="tpu_custom_call", output_to_operand_aliasing={{3}: (12, {}), {4}: (13, {})} | custom-call | flops 12999999488 | bytes 1000000 | tf_op jit(solution)/shard_map/feed/pallas_call | solution.py:227
  85.6 2.4 copy-done
  88.6 1.2 pad_maximum_fusion
  90.3 1.3 copy-done.19
  91.6 1.4 copy-done.21
  93.0 1.2 copy-done.23
  94.2 1.0 copy-done.33
  95.2 1.0 copy-done.35
  97.1 8.6 %back.3 = (bf16[144,384]{1,0:T(8,128)(2,1)S(1)}, bf16[144,384]{1,0:T(8,128)(2,1)S(1)}, bf16[144,384]{1,0:T(8,128)(2,1)S(1)}, bf16[144,384]{1,0:T(8,128)(2,1)S(1)...) custom-call(bf16[160,384]{1,0:T(8,128)(2,1)S(1)} %pad_maximum_fusion.21.refs_0_.refs_4_, ...), custom_call_target="tpu_custom_call" | custom-call | flops 8000000000 | bytes 1000000 | tf_op jit(solution)/shard_map/back/pallas_call | solution.py:316
  105.8 2.4 collective-permute-start.23
  109.0 1.6 bitcast_add_fusion
  111.8 3.9 %collective-permute-start.14 = (bf16[496,384]{1,0:T(8,128)(2,1)S(1)}, bf16[496,384]{1,0:T(8,128)(2,1)S(1)}, u32[]{:S(2)}, u32[]{:S(2)}) collective-permute-start(bf16[496,384]{1,0:T(8,128)(2,1)S(1)} %get-tuple-element.193), channel_id=1, source_target_pairs={{0,16},{4,20},{8,24},{12,28},{16,0},{20,4},{24,8},{28,12},{1,17},{... | collective-permute-start | bytes 1142792 | tf_op jit(solution)/shard_map/ppermute | solution.py:386
  115.8 9.0 %back.4 = (bf16[144,384]{1,0:T(8,128)(2,1)S(1)}, bf16[144,384]{1,0:T(8,128)(2,1)S(1)}, bf16[144,384]{1,0:T(8,128)(2,1)S(1)}, bf16[144,384]{1,0:T(8,128)(2,1)S(1)...) custom-call(bf16[144,384]{1,0:T(8,128)(2,1)S(1)} %get-tuple-element.177.refs_0_, ...), custom_call_target="tpu_custom_call", output_to_operand_aliasing={{4}: (12, {}), {5}: (13, {})} | custom-call | flops 8000000000 | bytes 1000000 | tf_op jit(solution)/shard_map/back/pallas_call | solution.py:316
  124.8 1.4 collective-permute-start.24
  126.3 6.3 %collective-permute-done.14 = bf16[496,384]{1,0:T(8,128)(2,1)S(1)} collective-permute-done((bf16[496,384]{1,0:T(8,128)(2,1)S(1)}, bf16[496,384]{1,0:T(8,128)(2,1)S(1)}, u32[]{:S(2)}, u32[]{:S(2)}) %collective-permute-start.14) | collective-permute-done | bytes 380960 | tf_op jit(solution)/shard_map/ppermute | solution.py:386
  132.5 1.1 collective-permute-start.25
  134.6 8.8 %back.5 = (bf16[144,384]{1,0:T(8,128)(2,1)S(1)}, bf16[144,384]{1,0:T(8,128)(2,1)S(1)}, bf16[144,384]{1,0:T(8,128)(2,1)S(1)}, bf16[144,384]{1,0:T(8,128)(2,1)S(1)...) custom-call(bf16[144,384]{1,0:T(8,128)(2,1)S(1)} %get-tuple-element.173.refs_0_, ...), custom_call_target="tpu_custom_call", output_to_operand_aliasing={{4}: (12, {}), {5}: (13, {})} | custom-call | flops 8000000000 | bytes 1000000 | tf_op jit(solution)/shard_map/back/pallas_call | solution.py:316
  143.7 2.5 %collective-permute-start.27 = (bf16[144,384]{1,0:T(8,128)(2,1)S(1)}, bf16[144,384]{1,0:T(8,128)(2,1)S(1)}, u32[]{:S(2)}, u32[]{:S(2)}) collective-permute-start(bf16[144,384]{1,0:T(8,128)(2,1)S(1)} %get-tuple-element.130), channel_id=1, source_target_pairs={{0,3},{1,2},{2,1},{3,0},{4,7},{5,6},{6,5},{7,4},{8,11},{9,10},{10,... | collective-permute-start | bytes 331784 | tf_op jit(solution)/shard_map/ppermute | solution.py:386
  146.4 1.9 collective-permute-start.16
  148.3 2.5 %collective-permute-start.18 = (bf16[160,384]{1,0:T(8,128)(2,1)S(1)}, bf16[160,384]{1,0:T(8,128)(2,1)S(1)}, u32[]{:S(2)}, u32[]{:S(2)}) collective-permute-start(bf16[160,384]{1,0:T(8,128)(2,1)S(1)} %get-tuple-element.191), channel_id=1, source_target_pairs={{0,3},{1,2},{2,1},{3,0},{4,7},{5,6},{6,5},{7,4},{8,11},{9,10},{10,... | collective-permute-start | bytes 368648 | tf_op jit(solution)/shard_map/ppermute | solution.py:386
  151.6 2.1 collective-permute-start.29
  153.7 1.1 collective-permute-done.28.refs_9_
  154.9 13.9 %collective-permute-done.29.refs_10_ = bf16[144,384]{1,0:T(8,128)(2,1)S(1)} collective-permute-done((bf16[144,384]{1,0:T(8,128)(2,1)S(1)}, bf16[144,384]{1,0:T(8,128)(2,1)S(1)}, u32[]{:S(2)}, u32[]{:S(2)}) %collective-permute-start.29) | collective-permute-done | bytes 110624 | tf_op jit(solution)/shard_map/ppermute | solution.py:386
  168.9 1.7 place.1
  170.6 1.8 collective-permute-start.19
  173.4 1.7 collective-permute-start.21
  176.4 1.6 collective-permute-done.19
  178.0 6.0 %collective-permute-done.20 = bf16[160,384]{1,0:T(8,128)(2,1)S(1)} collective-permute-done((bf16[160,384]{1,0:T(8,128)(2,1)S(1)}, bf16[160,384]{1,0:T(8,128)(2,1)S(1)}, u32[]{:S(2)}, u32[]{:S(2)}) %collective-permute-start.20) | collective-permute-done | bytes 122912 | tf_op jit(solution)/shard_map/ppermute | solution.py:386
  185.2 1.7 collective-permute-start.39
  189.1 1.7 collective-permute-start.33
  190.9 4.4 %collective-permute-done.38 = bf16[448,384]{1,0:T(8,128)(2,1)S(1)} collective-permute-done((bf16[448,384]{1,0:T(8,128)(2,1)S(1)}, bf16[448,384]{1,0:T(8,128)(2,1)S(1)}, u32[]{:S(2)}, u32[]{:S(2)}) %collective-permute-start.38) | collective-permute-done | bytes 344096 | tf_op jit(solution)/shard_map/ppermute | solution.py:386
  195.2 2.1 collective-permute-start.34
  197.4 5.2 %collective-permute-done.32 = bf16[176,384]{1,0:T(8,128)(2,1)S(1)} collective-permute-done((bf16[176,384]{1,0:T(8,128)(2,1)S(1)}, bf16[176,384]{1,0:T(8,128)(2,1)S(1)}, u32[]{:S(2)}, u32[]{:S(2)}) %collective-permute-start.32) | collective-permute-done | bytes 135200 | tf_op jit(solution)/shard_map/ppermute | solution.py:386
  202.6 1.3 collective-permute-done.33
  203.9 1.6 collective-permute-done.34
  205.7 3.7 %collective-permute-start.35 = (bf16[56,384]{1,0:T(8,128)(2,1)S(1)}, bf16[56,384]{1,0:T(8,128)(2,1)S(1)}, u32[]{:S(2)}, u32[]{:S(2)}) collective-permute-start(bf16[56,384]{1,0:T(8,128)(2,1)S(1)} %get-tuple-element.199), channel_id=1, source_target_pairs={{0,1},{1,0},{2,3},{3,2},{4,5},{5,4},{6,7},{7,6},{8,9},{9,8},{10,11... | collective-permute-start | bytes 129032 | tf_op jit(solution)/shard_map/ppermute | solution.py:386
  210.0 1.8 collective-permute-start.37
  211.9 2.5 %collective-permute-done.36 = bf16[56,384]{1,0:T(8,128)(2,1)S(1)} collective-permute-done((bf16[56,384]{1,0:T(8,128)(2,1)S(1)}, bf16[56,384]{1,0:T(8,128)(2,1)S(1)}, u32[]{:S(2)}, u32[]{:S(2)}) %collective-permute-start.36) | collective-permute-done | bytes 43040 | tf_op jit(solution)/shard_map/ppermute | solution.py:386
  214.3 1.6 collective-permute-done.37
  216.3 2.3 collective-permute-start.43
  218.5 2.1 collective-permute-start.44
  221.4 2.8 %collective-permute-done.44 = bf16[40,384]{1,0:T(8,128)(2,1)S(1)} collective-permute-done((bf16[40,384]{1,0:T(8,128)(2,1)S(1)}, bf16[40,384]{1,0:T(8,128)(2,1)S(1)}, u32[]{:S(2)}, u32[]{:S(2)}) %collective-permute-start.44) | collective-permute-done | bytes 30752 | tf_op jit(solution)/shard_map/ppermute | solution.py:386
  228.0 1.8 collective-permute-start.46
  229.8 1.2 collective-permute-start.47
  231.2 3.1 %collective-permute-done.46 = bf16[160,384]{1,0:T(8,128)(2,1)S(1)} collective-permute-done((bf16[160,384]{1,0:T(8,128)(2,1)S(1)}, bf16[160,384]{1,0:T(8,128)(2,1)S(1)}, u32[]{:S(2)}, u32[]{:S(2)}) %collective-permute-start.46) | collective-permute-done | bytes 122912 | tf_op jit(solution)/shard_map/ppermute | solution.py:386
  234.3 1.3 collective-permute-done.47
  235.7 1.6 convert_add_fusion
  239.3 4.9 %unpack.1 = (f32[1536,384]{1,0:T(8,128)}, f32[384,1536]{1,0:T(8,128)}, f32[384,384]{1,0:T(8,128)}, f32[384,1152]{1,0:T(8,128)}) custom-call(bf16[1792,384]{1,0:T(8,128)(2,1)S(1)} %bitcast.136, bf16[1792,384]{1,0:T(8,128)(2,1)S(1)} %collective-permute-done.41.refs_1_, bf16[640,384]{1,0:T(8,128)(2,1)S(1)} %bitcast.142, ...), custom_call_target="tpu_custom_call" | custom-call | tf_op jit(solution)/shard_map/unpack/pallas_call | solution.py:351
  (251 shorter events, 28.1 us)
Async XLA Ops:
  1.5 16.4 %copy-start.49 = (bf16[384]{0:T(512)(128)(2,1)S(1)}, bf16[384]{0:T(512)(128)(2,1)}, u32[]{:S(2)}) copy-start(bf16[384]{0:T(512)(128)(2,1)} %param.20) | copy-start | bytes 2308
  1.5 16.6 %copy-start.47 = (bf16[768]{0:T(1024)(128)(2,1)S(1)}, bf16[768]{0:T(1024)(128)(2,1)}, u32[]{:S(2)}) copy-start(bf16[768]{0:T(1024)(128)(2,1)} %param.22) | copy-start | bytes 4612
  1.5 16.8 %copy-start.50 = (bf16[384]{0:T(512)(128)(2,1)S(1)}, bf16[384]{0:T(512)(128)(2,1)}, u32[]{:S(2)}) copy-start(bf16[384]{0:T(512)(128)(2,1)} %param.24) | copy-start | bytes 2308
  1.5 17.0 %copy-start.51 = (bf16[384]{0:T(512)(128)(2,1)S(1)}, bf16[384]{0:T(512)(128)(2,1)}, u32[]{:S(2)}) copy-start(bf16[384]{0:T(512)(128)(2,1)} %param.25) | copy-start | bytes 2308
  1.5 17.2 %copy-start.52 = (bf16[384]{0:T(512)(128)(2,1)S(1)}, bf16[384]{0:T(512)(128)(2,1)}, u32[]{:S(2)}) copy-start(bf16[384]{0:T(512)(128)(2,1)} %param.26) | copy-start | bytes 2308
  1.5 17.5 %copy-start.53 = (bf16[384]{0:T(512)(128)(2,1)S(1)}, bf16[384]{0:T(512)(128)(2,1)}, u32[]{:S(2)}) copy-start(bf16[384]{0:T(512)(128)(2,1)} %param.30) | copy-start | bytes 2308
  1.5 17.7 %copy-start.46 = (bf16[1536]{0:T(1024)(128)(2,1)S(1)}, bf16[1536]{0:T(1024)(128)(2,1)}, u32[]{:S(2)}) copy-start(bf16[1536]{0:T(1024)(128)(2,1)} %param.28) | copy-start | bytes 9220
  1.6 22.9 %copy-start.3 = (bf16[384,1152]{1,0:T(8,128)(2,1)S(1)}, bf16[384,1152]{1,0:T(8,128)(2,1)}, u32[]{:S(2)}) copy-start(bf16[384,1152]{1,0:T(8,128)(2,1)} %refs_11_.11) | copy-start | bytes 2654212
  1.6 22.9 %copy-start.4 = (bf16[384,384]{1,0:T(8,128)(2,1)S(1)}, bf16[384,384]{1,0:T(8,128)(2,1)}, u32[]{:S(2)}) copy-start(bf16[384,384]{1,0:T(8,128)(2,1)} %refs_9_.11) | copy-start | bytes 884740
  3.9 16.0 %collective-permute-start = (bf16[160,384]{1,0:T(8,128)(2,1)S(1)}, bf16[160,384]{1,0:T(8,128)(2,1)S(1)}, u32[]{:S(2)}, u32[]{:S(2)}) collective-permute-start(bf16[160,384]{1,0:T(8,128)(2,1)S(1)} %pad_maximum_fusion.20), channel_id=1, source_target_pairs={{0,1},{1,0},{2,3},{3,2},{4,5},{5,4},{6,7},{7,6},{8,9},{9,8},{10,11... | collective-permute-start | bytes 368648 | tf_op jit(solution)/shard_map/ppermute | solution.py:386
  8.3 2.8 %collective-permute-start.9 = (f32[8,128]{1,0:T(8,128)S(1)}, f32[8,128]{1,0:T(8,128)S(1)}, u32[]{:S(2)}, u32[]{:S(2)}) collective-permute-start(f32[8,128]{1,0:T(8,128)S(1)} %broadcast_in_dim.71), channel_id=1, source_target_pairs={{0,4},{4,0},{8,12},{12,8},{16,20},{20,16},{24,28},{28,24},{1,5},{5... | collective-permute-start | bytes 12296 | tf_op jit(solution)/shard_map/ppermute | solution.py:386
  8.4 16.1 %collective-permute-start.5 = (bf16[160,384]{1,0:T(8,128)(2,1)S(1)}, bf16[160,384]{1,0:T(8,128)(2,1)S(1)}, u32[]{:S(2)}, u32[]{:S(2)}) collective-permute-start(bf16[160,384]{1,0:T(8,128)(2,1)S(1)} %pad_maximum_fusion.22), channel_id=1, source_target_pairs={{0,2},{1,3},{2,0},{3,1},{4,6},{5,7},{6,4},{7,5},{8,10},{9,11},{10,... | collective-permute-start | bytes 368648 | tf_op jit(solution)/shard_map/ppermute | solution.py:386
  11.7 3.7 %collective-permute-start.10 = (f32[8,128]{1,0:T(8,128)S(1)}, f32[8,128]{1,0:T(8,128)S(1)}, u32[]{:S(2)}, u32[]{:S(2)}) collective-permute-start(f32[8,128]{1,0:T(8,128)S(1)} %broadcast_add_fusion), channel_id=1, source_target_pairs={{0,8},{4,12},{8,0},{12,4},{16,24},{20,28},{24,16},{28,20},{1,9},{5... | collective-permute-start | bytes 12296 | tf_op jit(solution)/shard_map/ppermute | solution.py:386
  13.2 11.2 %collective-permute-start.6 = (bf16[160,384]{1,0:T(8,128)(2,1)S(1)}, bf16[160,384]{1,0:T(8,128)(2,1)S(1)}, u32[]{:S(2)}, u32[]{:S(2)}) collective-permute-start(bf16[160,384]{1,0:T(8,128)(2,1)S(1)} %pad_maximum_fusion.23), channel_id=1, source_target_pairs={{0,3},{1,2},{2,1},{3,0},{4,7},{5,6},{6,5},{7,4},{8,11},{9,10},{10,... | collective-permute-start | bytes 368648 | tf_op jit(solution)/shard_map/ppermute | solution.py:386
  16.0 3.9 %collective-permute-start.11 = (f32[8,128]{1,0:T(8,128)S(1)}, f32[8,128]{1,0:T(8,128)S(1)}, u32[]{:S(2)}, u32[]{:S(2)}) collective-permute-start(f32[8,128]{1,0:T(8,128)S(1)} %fusion.39), channel_id=1, source_target_pairs={{0,16},{4,20},{8,24},{12,28},{16,0},{20,4},{24,8},{28,12},{1,17},{... | collective-permute-start | bytes 12296 | tf_op jit(solution)/shard_map/ppermute | solution.py:386
  19.9 23.5 %collective-permute-start.1 = (bf16[144,384]{1,0:T(8,128)(2,1)S(1)}, bf16[144,384]{1,0:T(8,128)(2,1)S(1)}, u32[]{:S(2)}, u32[]{:S(2)}) collective-permute-start(bf16[144,384]{1,0:T(8,128)(2,1)S(1)} %get-tuple-element.83), channel_id=1, source_target_pairs={{0,1},{1,0},{2,3},{3,2},{4,5},{5,4},{6,7},{7,6},{8,9},{9,8},{10,11... | collective-permute-start | bytes 331784 | tf_op jit(solution)/shard_map/ppermute | solution.py:386
  20.4 27.5 %collective-permute-start.7 = (bf16[144,384]{1,0:T(8,128)(2,1)}, bf16[144,384]{1,0:T(8,128)(2,1)S(1)}, u32[]{:S(2)}, u32[]{:S(2)}) collective-permute-start(bf16[144,384]{1,0:T(8,128)(2,1)} %get-tuple-element.87), channel_id=1, source_target_pairs={{0,2},{1,3},{2,0},{3,1},{4,6},{5,7},{6,4},{7,5},{8,10},{9,11},{10,... | collective-permute-start | bytes 331784 | tf_op jit(solution)/shard_map/ppermute | solution.py:386
  22.4 25.5 %collective-permute-start.8 = (bf16[144,384]{1,0:T(8,128)(2,1)}, bf16[144,384]{1,0:T(8,128)(2,1)S(1)}, u32[]{:S(2)}, u32[]{:S(2)}) collective-permute-start(bf16[144,384]{1,0:T(8,128)(2,1)} %get-tuple-element.88), channel_id=1, source_target_pairs={{0,3},{1,2},{2,1},{3,0},{4,7},{5,6},{6,5},{7,4},{8,11},{9,10},{10,... | collective-permute-start | bytes 331784 | tf_op jit(solution)/shard_map/ppermute | solution.py:386
  43.5 22.7 %collective-permute-start.2 = (bf16[144,384]{1,0:T(8,128)(2,1)}, bf16[144,384]{1,0:T(8,128)(2,1)S(1)}, u32[]{:S(2)}, u32[]{:S(2)}) collective-permute-start(bf16[144,384]{1,0:T(8,128)(2,1)} %get-tuple-element.84), channel_id=1, source_target_pairs={{0,1},{1,0},{2,3},{3,2},{4,5},{5,4},{6,7},{7,6},{8,9},{9,8},{10,11... | collective-permute-start | bytes 331784 | tf_op jit(solution)/shard_map/ppermute | solution.py:386
  43.5 22.6 %collective-permute-start.3 = (bf16[144,384]{1,0:T(8,128)(2,1)}, bf16[144,384]{1,0:T(8,128)(2,1)S(1)}, u32[]{:S(2)}, u32[]{:S(2)}) collective-permute-start(bf16[144,384]{1,0:T(8,128)(2,1)} %get-tuple-element.85), channel_id=1, source_target_pairs={{0,2},{1,3},{2,0},{3,1},{4,6},{5,7},{6,4},{7,5},{8,10},{9,11},{10,... | collective-permute-start | bytes 331784 | tf_op jit(solution)/shard_map/ppermute | solution.py:386
  45.9 20.3 %collective-permute-start.4 = (bf16[144,384]{1,0:T(8,128)(2,1)S(1)}, bf16[144,384]{1,0:T(8,128)(2,1)S(1)}, u32[]{:S(2)}, u32[]{:S(2)}) collective-permute-start(bf16[144,384]{1,0:T(8,128)(2,1)S(1)} %copy-done.43), channel_id=1, source_target_pairs={{0,3},{1,2},{2,1},{3,0},{4,7},{5,6},{6,5},{7,4},{8,11},{9,10},{10,... | collective-permute-start | bytes 331784 | tf_op jit(solution)/shard_map/ppermute | solution.py:386
  89.8 18.4 %collective-permute-start.12 = (bf16[1840,384]{1,0:T(8,128)(2,1)}, bf16[1840,384]{1,0:T(8,128)(2,1)}, u32[]{:S(2)}, u32[]{:S(2)}) collective-permute-start(bf16[1840,384]{1,0:T(8,128)(2,1)} %pad_maximum_fusion), channel_id=1, source_target_pairs={{0,4},{4,0},{8,12},{12,8},{16,20},{20,16},{24,28},{28,24},{1,5},{5... | collective-permute-start | bytes 4239368 | tf_op jit(solution)/shard_map/ppermute | solution.py:386
  90.3 18.6 %slice-start = ((s8[5505024]{0:T(1024)(128)(4,1)}), s8[4194304]{0:T(1024)(128)(4,1)S(1)}, s32[]{:S(2)}) async-start(s8[5505024]{0:T(1024)(128)(4,1)} %bitcast.138), calls=%async_computation | async-start | bytes 8388608
  105.7 37.9 %collective-permute-start.22 = (bf16[144,384]{1,0:T(8,128)(2,1)S(1)}, bf16[144,384]{1,0:T(8,128)(2,1)S(1)}, u32[]{:S(2)}, u32[]{:S(2)}) collective-permute-start(bf16[144,384]{1,0:T(8,128)(2,1)S(1)} %get-tuple-element.116), channel_id=1, source_target_pairs={{0,1},{1,0},{2,3},{3,2},{4,5},{5,4},{6,7},{7,6},{8,9},{9,8},{10,11... | collective-permute-start | bytes 331784 | tf_op jit(solution)/shard_map/ppermute | solution.py:386
  105.8 40.4 %collective-permute-start.23 = (bf16[144,384]{1,0:T(8,128)(2,1)S(1)}, bf16[144,384]{1,0:T(8,128)(2,1)S(1)}, u32[]{:S(2)}, u32[]{:S(2)}) collective-permute-start(bf16[144,384]{1,0:T(8,128)(2,1)S(1)} %get-tuple-element.117), channel_id=1, source_target_pairs={{0,2},{1,3},{2,0},{3,1},{4,6},{5,7},{6,4},{7,5},{8,10},{9,11},{10,... | collective-permute-start | bytes 331784 | tf_op jit(solution)/shard_map/ppermute | solution.py:386
  110.9 13.9 %collective-permute-start.13 = (bf16[496,384]{1,0:T(8,128)(2,1)S(1)}, bf16[496,384]{1,0:T(8,128)(2,1)S(1)}, u32[]{:S(2)}, u32[]{:S(2)}) collective-permute-start(bf16[496,384]{1,0:T(8,128)(2,1)S(1)} %get-tuple-element.192), channel_id=1, source_target_pairs={{0,8},{4,12},{8,0},{12,4},{16,24},{20,28},{24,16},{28,20},{1,9},{5... | collective-permute-start | bytes 1142792 | tf_op jit(solution)/shard_map/ppermute | solution.py:386
  111.8 20.7 %collective-permute-start.14 = (bf16[496,384]{1,0:T(8,128)(2,1)S(1)}, bf16[496,384]{1,0:T(8,128)(2,1)S(1)}, u32[]{:S(2)}, u32[]{:S(2)}) collective-permute-start(bf16[496,384]{1,0:T(8,128)(2,1)S(1)} %get-tuple-element.193), channel_id=1, source_target_pairs={{0,16},{4,20},{8,24},{12,28},{16,0},{20,4},{24,8},{28,12},{1,17},{... | collective-permute-start | bytes 1142792 | tf_op jit(solution)/shard_map/ppermute | solution.py:386
  115.7 17.9 %collective-permute-start.15 = (bf16[496,384]{1,0:T(8,128)(2,1)S(1)}, bf16[496,384]{1,0:T(8,128)(2,1)S(1)}, u32[]{:S(2)}, u32[]{:S(2)}) collective-permute-start(bf16[496,384]{1,0:T(8,128)(2,1)S(1)} %get-tuple-element.194), channel_id=1, source_target_pairs={{0,24},{4,28},{8,16},{12,20},{16,8},{20,12},{24,0},{28,4},{1,25},{... | collective-permute-start | bytes 1142792 | tf_op jit(solution)/shard_map/ppermute | solution.py:386
  115.8 18.8 %copy-start.9 = (f32[576,384]{1,0:T(8,128)S(1)}, f32[576,384]{1,0:T(8,128)}, u32[]{:S(2)}) copy-start(f32[576,384]{1,0:T(8,128)} %copy-done.8) | copy-start | bytes 2654212
  115.8 18.8 %copy-start.11 = (bf16[576,768]{1,0:T(8,128)(2,1)S(1)}, bf16[576,768]{1,0:T(8,128)(2,1)}, u32[]{:S(2)}) copy-start(bf16[576,768]{1,0:T(8,128)(2,1)} %copy-done.10) | copy-start | bytes 2654212
  115.8 18.8 %copy-start.25 = (bf16[576,384]{1,0:T(8,128)(2,1)S(1)}, bf16[576,384]{1,0:T(8,128)(2,1)}, u32[]{:S(2)}) copy-start(bf16[576,384]{1,0:T(8,128)(2,1)} %copy-done.24) | copy-start | bytes 1327108
  115.8 18.8 %copy-start.27 = (bf16[576,384]{1,0:T(8,128)(2,1)S(1)}, bf16[576,384]{1,0:T(8,128)(2,1)}, u32[]{:S(2)}) copy-start(bf16[576,384]{1,0:T(8,128)(2,1)} %copy-done.26) | copy-start | bytes 1327108
  115.8 18.8 %copy-start.37 = (bf16[576,128]{1,0:T(8,128)(2,1)S(1)}, bf16[576,128]{1,0:T(8,128)(2,1)}, u32[]{:S(2)}) copy-start(bf16[576,128]{1,0:T(8,128)(2,1)} %copy-done.36) | copy-start | bytes 442372
  124.8 21.5 %collective-permute-start.24 = (bf16[144,384]{1,0:T(8,128)(2,1)S(1)}, bf16[144,384]{1,0:T(8,128)(2,1)S(1)}, u32[]{:S(2)}, u32[]{:S(2)}) collective-permute-start(bf16[144,384]{1,0:T(8,128)(2,1)S(1)} %get-tuple-element.118), channel_id=1, source_target_pairs={{0,3},{1,2},{2,1},{3,0},{4,7},{5,6},{6,5},{7,4},{8,11},{9,10},{10,... | collective-permute-start | bytes 331784 | tf_op jit(solution)/shard_map/ppermute | solution.py:386
  132.5 15.8 %collective-permute-start.25 = (bf16[144,384]{1,0:T(8,128)(2,1)S(1)}, bf16[144,384]{1,0:T(8,128)(2,1)S(1)}, u32[]{:S(2)}, u32[]{:S(2)}) collective-permute-start(bf16[144,384]{1,0:T(8,128)(2,1)S(1)} %get-tuple-element.128), channel_id=1, source_target_pairs={{0,1},{1,0},{2,3},{3,2},{4,5},{5,4},{6,7},{7,6},{8,9},{9,8},{10,11... | collective-permute-start | bytes 331784 | tf_op jit(solution)/shard_map/ppermute | solution.py:386
  133.6 14.7 %collective-permute-start.26 = (bf16[144,384]{1,0:T(8,128)(2,1)S(1)}, bf16[144,384]{1,0:T(8,128)(2,1)S(1)}, u32[]{:S(2)}, u32[]{:S(2)}) collective-permute-start(bf16[144,384]{1,0:T(8,128)(2,1)S(1)} %get-tuple-element.129), channel_id=1, source_target_pairs={{0,2},{1,3},{2,0},{3,1},{4,6},{5,7},{6,4},{7,5},{8,10},{9,11},{10,... | collective-permute-start | bytes 331784 | tf_op jit(solution)/shard_map/ppermute | solution.py:386
  143.7 8.0 %collective-permute-start.27 = (bf16[144,384]{1,0:T(8,128)(2,1)S(1)}, bf16[144,384]{1,0:T(8,128)(2,1)S(1)}, u32[]{:S(2)}, u32[]{:S(2)}) collective-permute-start(bf16[144,384]{1,0:T(8,128)(2,1)S(1)} %get-tuple-element.130), channel_id=1, source_target_pairs={{0,3},{1,2},{2,1},{3,0},{4,7},{5,6},{6,5},{7,4},{8,11},{9,10},{10,... | collective-permute-start | bytes 331784 | tf_op jit(solution)/shard_map/ppermute | solution.py:386
  146.2 8.7 %collective-permute-start.28 = (bf16[144,384]{1,0:T(8,128)(2,1)S(1)}, bf16[144,384]{1,0:T(8,128)(2,1)S(1)}, u32[]{:S(2)}, u32[]{:S(2)}) collective-permute-start(bf16[144,384]{1,0:T(8,128)(2,1)S(1)} %get-tuple-element.140), channel_id=1, source_target_pairs={{0,1},{1,0},{2,3},{3,2},{4,5},{5,4},{6,7},{7,6},{8,9},{9,8},{10,11... | collective-permute-start | bytes 331784 | tf_op jit(solution)/shard_map/ppermute | solution.py:386
  146.4 24.2 %collective-permute-start.16 = (bf16[160,384]{1,0:T(8,128)(2,1)S(1)}, bf16[160,384]{1,0:T(8,128)(2,1)S(1)}, u32[]{:S(2)}, u32[]{:S(2)}) collective-permute-start(bf16[160,384]{1,0:T(8,128)(2,1)S(1)} %get-tuple-element.189), channel_id=1, source_target_pairs={{0,1},{1,0},{2,3},{3,2},{4,5},{5,4},{6,7},{7,6},{8,9},{9,8},{10,11... | collective-permute-start | bytes 368648 | tf_op jit(solution)/shard_map/ppermute | solution.py:386
  148.3 22.2 %collective-permute-start.17 = (bf16[160,384]{1,0:T(8,128)(2,1)S(1)}, bf16[160,384]{1,0:T(8,128)(2,1)S(1)}, u32[]{:S(2)}, u32[]{:S(2)}) collective-permute-start(bf16[160,384]{1,0:T(8,128)(2,1)S(1)} %get-tuple-element.190), channel_id=1, source_target_pairs={{0,2},{1,3},{2,0},{3,1},{4,6},{5,7},{6,4},{7,5},{8,10},{9,11},{10,... | collective-permute-start | bytes 368648 | tf_op jit(solution)/shard_map/ppermute | solution.py:386
  148.3 22.2 %collective-permute-start.18 = (bf16[160,384]{1,0:T(8,128)(2,1)S(1)}, bf16[160,384]{1,0:T(8,128)(2,1)S(1)}, u32[]{:S(2)}, u32[]{:S(2)}) collective-permute-start(bf16[160,384]{1,0:T(8,128)(2,1)S(1)} %get-tuple-element.191), channel_id=1, source_target_pairs={{0,3},{1,2},{2,1},{3,0},{4,7},{5,6},{6,5},{7,4},{8,11},{9,10},{10,... | collective-permute-start | bytes 368648 | tf_op jit(solution)/shard_map/ppermute | solution.py:386
  151.6 17.2 %collective-permute-start.29 = (bf16[144,384]{1,0:T(8,128)(2,1)S(1)}, bf16[144,384]{1,0:T(8,128)(2,1)S(1)}, u32[]{:S(2)}, u32[]{:S(2)}) collective-permute-start(bf16[144,384]{1,0:T(8,128)(2,1)S(1)} %get-tuple-element.141), channel_id=1, source_target_pairs={{0,2},{1,3},{2,0},{3,1},{4,6},{5,7},{6,4},{7,5},{8,10},{9,11},{10,... | collective-permute-start | bytes 331784 | tf_op jit(solution)/shard_map/ppermute | solution.py:386
  154.9 14.0 %collective-permute-start.30 = (bf16[144,384]{1,0:T(8,128)(2,1)S(1)}, bf16[144,384]{1,0:T(8,128)(2,1)S(1)}, u32[]{:S(2)}, u32[]{:S(2)}) collective-permute-start(bf16[144,384]{1,0:T(8,128)(2,1)S(1)} %get-tuple-element.142), channel_id=1, source_target_pairs={{0,3},{1,2},{2,1},{3,0},{4,7},{5,6},{6,5},{7,4},{8,11},{9,10},{10,... | collective-permute-start | bytes 331784 | tf_op jit(solution)/shard_map/ppermute | solution.py:386
  168.9 19.1 %collective-permute-start.31 = (bf16[656,384]{1,0:T(8,128)(2,1)S(1)}, bf16[656,384]{1,0:T(8,128)(2,1)S(1)}, u32[]{:S(2)}, u32[]{:S(2)}) collective-permute-start(bf16[656,384]{1,0:T(8,128)(2,1)S(1)} %pad_maximum_fusion.7), channel_id=1, source_target_pairs={{0,4},{4,0},{8,12},{12,8},{16,20},{20,16},{24,28},{28,24},{1,5},{5... | collective-permute-start | bytes 1511432 | tf_op jit(solution)/shard_map/ppermute | solution.py:386
  170.6 7.3 %collective-permute-start.19 = (bf16[160,384]{1,0:T(8,128)(2,1)S(1)}, bf16[160,384]{1,0:T(8,128)(2,1)S(1)}, u32[]{:S(2)}, u32[]{:S(2)}) collective-permute-start(bf16[160,384]{1,0:T(8,128)(2,1)S(1)} %pad_maximum_fusion.24), channel_id=1, source_target_pairs={{0,1},{1,0},{2,3},{3,2},{4,5},{5,4},{6,7},{7,6},{8,9},{9,8},{10,11... | collective-permute-start | bytes 368648 | tf_op jit(solution)/shard_map/ppermute | solution.py:386
  172.5 11.6 %collective-permute-start.20 = (bf16[160,384]{1,0:T(8,128)(2,1)S(1)}, bf16[160,384]{1,0:T(8,128)(2,1)S(1)}, u32[]{:S(2)}, u32[]{:S(2)}) collective-permute-start(bf16[160,384]{1,0:T(8,128)(2,1)S(1)} %pad_maximum_fusion.24), channel_id=1, source_target_pairs={{0,2},{1,3},{2,0},{3,1},{4,6},{5,7},{6,4},{7,5},{8,10},{9,11},{10,... | collective-permute-start | bytes 368648 | tf_op jit(solution)/shard_map/ppermute | solution.py:386
  173.4 10.6 %collective-permute-start.21 = (bf16[160,384]{1,0:T(8,128)(2,1)S(1)}, bf16[160,384]{1,0:T(8,128)(2,1)S(1)}, u32[]{:S(2)}, u32[]{:S(2)}) collective-permute-start(bf16[160,384]{1,0:T(8,128)(2,1)S(1)} %pad_maximum_fusion.24), channel_id=1, source_target_pairs={{0,3},{1,2},{2,1},{3,0},{4,7},{5,6},{6,5},{7,4},{8,11},{9,10},{10,... | collective-permute-start | bytes 368648 | tf_op jit(solution)/shard_map/ppermute | solution.py:386
  184.2 11.1 %collective-permute-start.38 = (bf16[448,384]{1,0:T(8,128)(2,1)S(1)}, bf16[448,384]{1,0:T(8,128)(2,1)S(1)}, u32[]{:S(2)}, u32[]{:S(2)}) collective-permute-start(bf16[448,384]{1,0:T(8,128)(2,1)S(1)} %bitcast.154), channel_id=1, source_target_pairs={{0,8},{4,12},{8,0},{12,4},{16,24},{20,28},{24,16},{28,20},{1,9},{5... | collective-permute-start | bytes 1032200 | tf_op jit(solution)/shard_map/ppermute | solution.py:386
  185.2 26.6 %collective-permute-start.39 = (bf16[448,384]{1,0:T(8,128)(2,1)S(1)}, bf16[448,384]{1,0:T(8,128)(2,1)S(1)}, u32[]{:S(2)}, u32[]{:S(2)}) collective-permute-start(bf16[448,384]{1,0:T(8,128)(2,1)S(1)} %bitcast.155), channel_id=1, source_target_pairs={{0,16},{4,20},{8,24},{12,28},{16,0},{20,4},{24,8},{28,12},{1,17},{... | collective-permute-start | bytes 1032200 | tf_op jit(solution)/shard_map/ppermute | solution.py:386
  186.9 29.3 %collective-permute-start.40 = (bf16[448,384]{1,0:T(8,128)(2,1)S(1)}, bf16[448,384]{1,0:T(8,128)(2,1)S(1)}, u32[]{:S(2)}, u32[]{:S(2)}) collective-permute-start(bf16[448,384]{1,0:T(8,128)(2,1)S(1)} %bitcast.156), channel_id=1, source_target_pairs={{0,24},{4,28},{8,16},{12,20},{16,8},{20,12},{24,0},{28,4},{1,25},{... | collective-permute-start | bytes 1032200 | tf_op jit(solution)/shard_map/ppermute | solution.py:386
  188.3 14.3 %collective-permute-start.32 = (bf16[176,384]{1,0:T(8,128)(2,1)S(1)}, bf16[176,384]{1,0:T(8,128)(2,1)S(1)}, u32[]{:S(2)}, u32[]{:S(2)}) collective-permute-start(bf16[176,384]{1,0:T(8,128)(2,1)S(1)} %get-tuple-element.202), channel_id=1, source_target_pairs={{0,8},{4,12},{8,0},{12,4},{16,24},{20,28},{24,16},{28,20},{1,9},{5... | collective-permute-start | bytes 405512 | tf_op jit(solution)/shard_map/ppermute | solution.py:386
  189.1 14.8 %collective-permute-start.33 = (bf16[176,384]{1,0:T(8,128)(2,1)S(1)}, bf16[176,384]{1,0:T(8,128)(2,1)S(1)}, u32[]{:S(2)}, u32[]{:S(2)}) collective-permute-start(bf16[176,384]{1,0:T(8,128)(2,1)S(1)} %get-tuple-element.203), channel_id=1, source_target_pairs={{0,16},{4,20},{8,24},{12,28},{16,0},{20,4},{24,8},{28,12},{1,17},{... | collective-permute-start | bytes 405512 | tf_op jit(solution)/shard_map/ppermute | solution.py:386
  195.2 10.3 %collective-permute-start.34 = (bf16[176,384]{1,0:T(8,128)(2,1)S(1)}, bf16[176,384]{1,0:T(8,128)(2,1)S(1)}, u32[]{:S(2)}, u32[]{:S(2)}) collective-permute-start(bf16[176,384]{1,0:T(8,128)(2,1)S(1)} %get-tuple-element.204), channel_id=1, source_target_pairs={{0,24},{4,28},{8,16},{12,20},{16,8},{20,12},{24,0},{28,4},{1,25},{... | collective-permute-start | bytes 405512 | tf_op jit(solution)/shard_map/ppermute | solution.py:386
  205.7 6.2 %collective-permute-start.35 = (bf16[56,384]{1,0:T(8,128)(2,1)S(1)}, bf16[56,384]{1,0:T(8,128)(2,1)S(1)}, u32[]{:S(2)}, u32[]{:S(2)}) collective-permute-start(bf16[56,384]{1,0:T(8,128)(2,1)S(1)} %get-tuple-element.199), channel_id=1, source_target_pairs={{0,1},{1,0},{2,3},{3,2},{4,5},{5,4},{6,7},{7,6},{8,9},{9,8},{10,11... | collective-permute-start | bytes 129032 | tf_op jit(solution)/shard_map/ppermute | solution.py:386
  209.3 5.0 %collective-permute-start.36 = (bf16[56,384]{1,0:T(8,128)(2,1)S(1)}, bf16[56,384]{1,0:T(8,128)(2,1)S(1)}, u32[]{:S(2)}, u32[]{:S(2)}) collective-permute-start(bf16[56,384]{1,0:T(8,128)(2,1)S(1)} %get-tuple-element.200), channel_id=1, source_target_pairs={{0,2},{1,3},{2,0},{3,1},{4,6},{5,7},{6,4},{7,5},{8,10},{9,11},{10,... | collective-permute-start | bytes 129032 | tf_op jit(solution)/shard_map/ppermute | solution.py:386
  210.0 5.9 %collective-permute-start.37 = (bf16[56,384]{1,0:T(8,128)(2,1)S(1)}, bf16[56,384]{1,0:T(8,128)(2,1)S(1)}, u32[]{:S(2)}, u32[]{:S(2)}) collective-permute-start(bf16[56,384]{1,0:T(8,128)(2,1)S(1)} %get-tuple-element.201), channel_id=1, source_target_pairs={{0,3},{1,2},{2,1},{3,0},{4,7},{5,6},{6,5},{7,4},{8,11},{9,10},{10,... | collective-permute-start | bytes 129032 | tf_op jit(solution)/shard_map/ppermute | solution.py:386
  215.9 4.7 %collective-permute-start.42 = (bf16[40,384]{1,0:T(8,128)(2,1)S(1)}, bf16[40,384]{1,0:T(8,128)(2,1)S(1)}, u32[]{:S(2)}, u32[]{:S(2)}) collective-permute-start(bf16[40,384]{1,0:T(8,128)(2,1)S(1)} %get-tuple-element.156), channel_id=1, source_target_pairs={{0,1},{1,0},{2,3},{3,2},{4,5},{5,4},{6,7},{7,6},{8,9},{9,8},{10,11... | collective-permute-start | bytes 92168 | tf_op jit(solution)/shard_map/ppermute | solution.py:386
  216.2 23.1 %collective-permute-start.41 = (bf16[1792,384]{1,0:T(8,128)(2,1)S(1)}, bf16[1792,384]{1,0:T(8,128)(2,1)S(1)}, u32[]{:S(2)}, u32[]{:S(2)}) collective-permute-start(bf16[1792,384]{1,0:T(8,128)(2,1)S(1)} %bitcast.135), channel_id=1, source_target_pairs={{0,4},{4,0},{8,12},{12,8},{16,20},{20,16},{24,28},{28,24},{1,5},{5... | collective-permute-start | bytes 4128776 | tf_op jit(solution)/shard_map/ppermute | solution.py:386
  216.3 5.1 %collective-permute-start.43 = (bf16[40,384]{1,0:T(8,128)(2,1)S(1)}, bf16[40,384]{1,0:T(8,128)(2,1)S(1)}, u32[]{:S(2)}, u32[]{:S(2)}) collective-permute-start(bf16[40,384]{1,0:T(8,128)(2,1)S(1)} %get-tuple-element.156), channel_id=1, source_target_pairs={{0,2},{1,3},{2,0},{3,1},{4,6},{5,7},{6,4},{7,5},{8,10},{9,11},{10,... | collective-permute-start | bytes 92168 | tf_op jit(solution)/shard_map/ppermute | solution.py:386
  218.5 5.7 %collective-permute-start.44 = (bf16[40,384]{1,0:T(8,128)(2,1)S(1)}, bf16[40,384]{1,0:T(8,128)(2,1)S(1)}, u32[]{:S(2)}, u32[]{:S(2)}) collective-permute-start(bf16[40,384]{1,0:T(8,128)(2,1)S(1)} %get-tuple-element.156), channel_id=1, source_target_pairs={{0,3},{1,2},{2,1},{3,0},{4,7},{5,6},{6,5},{7,4},{8,11},{9,10},{10,... | collective-permute-start | bytes 92168 | tf_op jit(solution)/shard_map/ppermute | solution.py:386
  224.3 6.9 %collective-permute-start.45 = (bf16[160,384]{1,0:T(8,128)(2,1)S(1)}, bf16[160,384]{1,0:T(8,128)(2,1)S(1)}, u32[]{:S(2)}, u32[]{:S(2)}) collective-permute-start(bf16[160,384]{1,0:T(8,128)(2,1)S(1)} %bitcast.161), channel_id=1, source_target_pairs={{0,8},{4,12},{8,0},{12,4},{16,24},{20,28},{24,16},{28,20},{1,9},{5... | collective-permute-start | bytes 368648 | tf_op jit(solution)/shard_map/ppermute | solution.py:386
  228.0 6.3 %collective-permute-start.46 = (bf16[160,384]{1,0:T(8,128)(2,1)S(1)}, bf16[160,384]{1,0:T(8,128)(2,1)S(1)}, u32[]{:S(2)}, u32[]{:S(2)}) collective-permute-start(bf16[160,384]{1,0:T(8,128)(2,1)S(1)} %bitcast.162), channel_id=1, source_target_pairs={{0,16},{4,20},{8,24},{12,28},{16,0},{20,4},{24,8},{28,12},{1,17},{... | collective-permute-start | bytes 368648 | tf_op jit(solution)/shard_map/ppermute | solution.py:386
  229.8 5.8 %collective-permute-start.47 = (bf16[160,384]{1,0:T(8,128)(2,1)S(1)}, bf16[160,384]{1,0:T(8,128)(2,1)S(1)}, u32[]{:S(2)}, u32[]{:S(2)}) collective-permute-start(bf16[160,384]{1,0:T(8,128)(2,1)S(1)} %bitcast.163), channel_id=1, source_target_pairs={{0,24},{4,28},{8,16},{12,20},{16,8},{20,12},{24,0},{28,4},{1,25},{... | collective-permute-start | bytes 368648 | tf_op jit(solution)/shard_map/ppermute | solution.py:386
  235.6 3.7 %collective-permute-start.48 = (bf16[640,384]{1,0:T(8,128)(2,1)S(1)}, bf16[640,384]{1,0:T(8,128)(2,1)}, u32[]{:S(2)}, u32[]{:S(2)}) collective-permute-start(bf16[640,384]{1,0:T(8,128)(2,1)S(1)} %bitcast.141), channel_id=1, source_target_pairs={{0,4},{4,0},{8,12},{12,8},{16,20},{20,16},{24,28},{28,24},{1,5},{5... | collective-permute-start | bytes 1474568 | tf_op jit(solution)/shard_map/ppermute | solution.py:386
  (42 other events, 281.7 us)
